TPU v7x, 32 devices: a whole 2x2x4 slice. The times are simulated.
32 devices in a mesh: grp: 2 (over x), lat: 16 (over z, y, core).
Axes of the slice: x: 2, y: 2, z: 4, core: 2. Of those that a mesh axis runs over, the one named last changes fastest.
Arguments:
- gauge: float32 [4, 2, 3, 3, 16, 4, 256], P(None, None, None, None, 'lat', 'grp'), may hold values from -2.5 to 2.5
- amplitudes: float32 [2, 2, 3, 16, 32], P(None, None, None, 'lat'), may hold values from -600 to 600
- source_sites: int32 [2, 16, 32], P(None, 'lat'), may hold values from 0 to 1023
- spin_weights: float32 [2, 2, 4], replicated, may hold values from -4 to 4
Outputs:
- propagator: float32 [2, 2, 4, 3, 16, 4, 256], P(None, None, None, None, 'lat', 'grp')
Inputs may be any that keep to these rules, and one draw needn't show every extreme that they name: source_sites[r, t, p] is the spatial site z * 16 * 16 + y * 16 + x of point p of side r on time slice t; points may coincide.
All inputs are finite; a program needn't handle non-finite values.
Results may differ from a plain program's by a relative error of at most 0.0001.
Values sent between devices are 32-bit elements; how exact they have to be, the bound alone decides.
A program may use at most 64 MiB of HBM per device.

v0:
```python
import jax
import jax.numpy as jnp
from jax import lax
from jax.sharding import PartitionSpec as P

LXY = 16
N_SMEAR = 4
ITERS = 4


smear_weight = 0.2
hop_kappa = 0.125
gamma_perm = ((3, 2, 1, 0), (3, 2, 1, 0), (2, 3, 0, 1), (2, 3, 0, 1))
gamma_phase = ((1, 1, 3, 3), (2, 0, 0, 2), (1, 3, 3, 1), (0, 0, 0, 0))


def passed_along(array, axis, by):
    size = lax.axis_size(axis)
    return lax.ppermute(array, axis, [(i, (i + by) % size) for i in range(size)])


def extended(array, sides, width):
    for axis, dim in sides:
        size, length = (lax.axis_size(axis), array.shape[dim])
        up = [(i, (i + 1) % size) for i in range(size)]
        down = [(j, i) for i, j in up]
        last = lax.slice_in_dim(array, length - width, length, axis=dim)
        first = lax.slice_in_dim(array, 0, width, axis=dim)
        before = lax.ppermute(last, axis, up)
        after = lax.ppermute(first, axis, down)
        array = jnp.concatenate([before, array, after], axis=dim)
    return array


def phase_times(code, real, imag):
    if code == 0:
        return (real, imag)
    if code == 1:
        return (-imag, real)
    if code == 2:
        return (-real, -imag)
    return (imag, -real)


def apply_gamma(hop_dir, field):
    rows_re = []
    rows_im = []
    for spin in range(4):
        picked = field[:, :, gamma_perm[hop_dir][spin]]
        real, imag = phase_times(gamma_phase[hop_dir][spin], picked[:, 0], picked[:, 1])
        rows_re.append(real)
        rows_im.append(imag)
    return jnp.stack([jnp.stack(rows_re, 1), jnp.stack(rows_im, 1)], 1)


def colour_times(links, field):
    link_re = links[0][None, None]
    link_im = links[1][None, None]
    field_re = field[:, 0][:, :, None]
    field_im = field[:, 1][:, :, None]
    out_re = jnp.sum(link_re * field_re - link_im * field_im, axis=3)
    out_im = jnp.sum(link_re * field_im + link_im * field_re, axis=3)
    return jnp.stack([out_re, out_im], 1)


def adjoint(links):
    return jnp.stack([jnp.swapaxes(links[0], 0, 1), -jnp.swapaxes(links[1], 0, 1)])


def roll_site(field, hop_dir, offset):
    if hop_dir == 1:
        return jnp.roll(field, offset * LXY, axis=-1)
    column = lax.broadcasted_iota(jnp.int32, (field.shape[-1],), 0) % LXY
    if offset < 0:
        return jnp.where(
            column == LXY - 1, jnp.roll(field, LXY - 1, axis=-1), jnp.roll(field, -1, axis=-1)
        )
    return jnp.where(column == 0, jnp.roll(field, 1 - LXY, axis=-1), jnp.roll(field, 1, axis=-1))


def build_source(amps, sites, offset, count, plane):
    cells = offset + lax.broadcasted_iota(jnp.int32, (1, 1, 1, count), 3)
    marks = (sites[..., None] == cells).astype(amps.dtype)
    flat = jnp.einsum("rkctp,rtpq->rkctq", amps, marks, precision=lax.Precision.HIGHEST)
    shape = flat.shape
    return flat.reshape((shape[0], 2, 1, 3, shape[3], count // plane, plane))


def spin_expand(colour_field, weights):
    weight_re = weights[:, 0][:, :, None, None, None, None]
    weight_im = weights[:, 1][:, :, None, None, None, None]
    field_re = colour_field[:, 0]
    field_im = colour_field[:, 1]
    out_re = weight_re * field_re - weight_im * field_im
    out_im = weight_re * field_im + weight_im * field_re
    return jnp.stack([out_re, out_im], 1)


def plane_terms(spinor, links, link_adjs, dirs):
    total = jnp.zeros_like(spinor)
    for hop_dir in range(dirs):
        forward = colour_times(links[hop_dir], roll_site(spinor, hop_dir, -1))
        total = total + forward - apply_gamma(hop_dir, forward)
        back = roll_site(colour_times(link_adjs[hop_dir], spinor), hop_dir, 1)
        total = total + back + apply_gamma(hop_dir, back)
    return total


def time_terms(spinor, time_links, time_adj, sign_low, sign_high):
    slab_time = spinor.shape[4]
    upper = spinor[:, :, :2]
    lower = spinor[:, :, 2:]
    minus_half = upper - lower
    plus_half = colour_times(time_adj, upper + lower)
    arriving = passed_along(minus_half, "lat", -1)
    leaving = passed_along(plus_half, "lat", 1)
    ahead = jnp.concatenate([minus_half[:, :, :, :, 1:], sign_high * arriving], axis=4)
    behind = jnp.concatenate([sign_low * leaving, plus_half[:, :, :, :, : slab_time - 1]], axis=4)
    forward = colour_times(time_links, ahead)
    total = jnp.concatenate([forward, -forward], axis=2)
    return total + jnp.concatenate([behind, behind], axis=2)


def on_device(gauge, amplitudes, source_sites, spin_weights):
    group = lax.axis_index("grp")
    sheets = lax.axis_size("lat")
    sheet = lax.axis_index("lat")
    thick = gauge.shape[5]
    plane = gauge.shape[6]
    z_links = gauge[2]
    z_rim = passed_along(z_links[:, :, :, :, thick - 1 :], "grp", 1)
    z_behind = adjoint(jnp.concatenate([z_rim, z_links[:, :, :, :, : thick - 1]], axis=4))
    local_links = [gauge[hop_dir] for hop_dir in range(4)]
    local_adjs = [adjoint(local_links[hop_dir]) for hop_dir in range(4)]
    colour_field = build_source(
        amplitudes, source_sites, group * thick * plane, thick * plane, plane
    )
    for smear_index in range(N_SMEAR):
        padded = extended(colour_field, (("grp", 5),), 1)
        total = colour_field
        for hop_dir in range(2):
            total = total + smear_weight * colour_times(
                local_links[hop_dir], roll_site(colour_field, hop_dir, -1)
            )
            total = total + smear_weight * roll_site(
                colour_times(local_adjs[hop_dir], colour_field), hop_dir, 1
            )
        total = total + smear_weight * colour_times(z_links, padded[:, :, :, :, :, 2:])
        total = total + smear_weight * colour_times(z_behind, padded[:, :, :, :, :, :thick])
        colour_field = total / (1.0 + 6.0 * smear_weight)
    sign_low = jnp.where(sheet == 0, -1.0, 1.0).astype(jnp.float32)
    sign_high = jnp.where(sheet == sheets - 1, -1.0, 1.0).astype(jnp.float32)
    source = spin_expand(colour_field, spin_weights)
    spinor = source
    for iteration in range(ITERS):
        total = plane_terms(spinor, local_links, local_adjs, 2)
        padded = extended(spinor, (("grp", 5),), 1)
        forward = colour_times(z_links, padded[:, :, :, :, :, 2:])
        total = total + forward - apply_gamma(2, forward)
        back = colour_times(z_behind, padded[:, :, :, :, :, :thick])
        total = total + back + apply_gamma(2, back)
        total = total + time_terms(spinor, local_links[3], local_adjs[3], sign_low, sign_high)
        spinor = source + hop_kappa * total
    return spinor


def solution(mesh):
    placed = (
        P(None, None, None, None, "lat", "grp", None),
        P(None, None, None, "lat", None),
        P(None, "lat", None),
        P(),
    )
    return jax.shard_map(
        on_device,
        mesh=mesh,
        in_specs=placed,
        out_specs=P(None, None, None, None, "lat", "grp", None),
        check_vma=False,
    )
```

profile of v0, /device:TPU:0, one launch (start us, length us, event | category | flops | bytes accessed | tf_op | source)
XLA Modules:
  0.0 80.0 jit_solution(2200242138106772113)
XLA Ops:
  0.0 0.7 copy-done.3
  0.7 0.9 %convolution_bitcast_fusion = f32[2,2,3,1,512]{4,2,1,0,3:T(4,128)S(1)} fusion(s32[512]{0:T(512)S(1)} %iota_add_fusion, s32[2,32]{1,0:T(2,128)} %bitcast.1050, f32[2,2,3,32]{3,1,2,0:T(2,128)S(1)} %bitcast.1049), kind=kOutput, calls=%fused_computation | convolution fusion | flops 2392064 | bytes 28416 | tf_op jit(solution)/shard_map/rkctp,rtpq->rkctq/dot_general | solution.py:84
  1.7 3.0 %collective-permute-start = (f32[2,2,1,3,1,1,256]{6,5,1,3,0,4,2:T(1,128)S(1)}, f32[2,2,1,3,1,1,256]{6,5,1,3,0,4,2:T(1,128)S(1)}, u32[]{:S(2)}, u32[]{:S(2)}) collective-permute-start(f32[2,2,1,3,1,1,256]{6,5,1,3,0,4,2:T(1,128)S(1)} %get-tuple-element.597), channel_id=1, source_target_pairs={{16,0},{0,16},{17,1},{1,17},{18,2},{2,18},{19,3},{3,19},{20,4},{4,... | collective-permute-start | bytes 36872 | tf_op jit(solution)/shard_map/ppermute | solution.py:30
  4.8 2.0 %collective-permute-start.1 = (f32[2,3,3,1,1,256]{5,4,2,1,0,3:T(1,128)S(1)}, f32[2,3,3,1,1,256]{5,4,2,1,0,3:T(1,128)S(1)}, u32[]{:S(2)}, u32[]{:S(2)}) collective-permute-start(f32[2,3,3,1,1,256]{5,4,2,1,0,3:T(1,128)S(1)} %get-tuple-element.349), channel_id=1, source_target_pairs={{0,16},{16,0},{1,17},{17,1},{2,18},{18,2},{3,19},{19,3},{4,20},{20... | collective-permute-start | bytes 55304 | tf_op jit(solution)/shard_map/ppermute | solution.py:19
  7.2 0.7 slice-done
  10.6 0.8 %collective-permute-start.3 = (f32[2,2,1,3,1,1,256]{6,5,3,0,4,2,1:T(1,128)S(1)}, f32[2,2,1,3,1,1,256]{6,5,3,0,4,2,1:T(1,128)S(1)}, u32[]{:S(2)}, u32[]{:S(2)}) collective-permute-start(f32[2,2,1,3,1,1,256]{6,5,3,0,4,2,1:T(1,128)S(1)} %get-tuple-element.589), channel_id=1, source_target_pairs={{16,0},{0,16},{17,1},{1,17},{18,2},{2,18},{19,3},{3,19},{20,4},{4,... | collective-permute-start | bytes 36872 | tf_op jit(solution)/shard_map/ppermute | solution.py:30
  11.4 1.3 %collective-permute-start.4 = (f32[2,2,1,3,1,1,256]{6,5,3,0,4,2,1:T(1,128)S(1)}, f32[2,2,1,3,1,1,256]{6,5,3,0,4,2,1:T(1,128)S(1)}, u32[]{:S(2)}, u32[]{:S(2)}) collective-permute-start(f32[2,2,1,3,1,1,256]{6,5,3,0,4,2,1:T(1,128)S(1)} %get-tuple-element.590), channel_id=1, source_target_pairs={{0,16},{16,0},{1,17},{17,1},{2,18},{18,2},{3,19},{19,3},{4,20},{20... | collective-permute-start | bytes 36872 | tf_op jit(solution)/shard_map/ppermute | solution.py:29
  12.9 1.5 %collective-permute-done.3 = f32[2,2,1,3,1,1,256]{6,5,3,0,4,2,1:T(1,128)S(1)} collective-permute-done((f32[2,2,1,3,1,1,256]{6,5,3,0,4,2,1:T(1,128)S(1)}, f32[2,2,1,3,1,1,256]{6,5,3,0,4,2,1:T(1,128)S(1)}, u32[]{:S(2)}, u32[]{:S(2)}) %collective-permute-start.3) | collective-permute-done | bytes 12320 | tf_op jit(solution)/shard_map/ppermute | solution.py:30
  14.4 0.7 collective-permute-done.4
  16.3 1.4 %collective-permute-start.5 = (f32[2,2,1,3,1,1,256]{6,5,3,0,4,2,1:T(1,128)S(1)}, f32[2,2,1,3,1,1,256]{6,5,3,0,4,2,1:T(1,128)S(1)}, u32[]{:S(2)}, u32[]{:S(2)}) collective-permute-start(f32[2,2,1,3,1,1,256]{6,5,3,0,4,2,1:T(1,128)S(1)} %get-tuple-element.581), channel_id=1, source_target_pairs={{16,0},{0,16},{17,1},{1,17},{18,2},{2,18},{19,3},{3,19},{20,4},{4,... | collective-permute-start | bytes 36872 | tf_op jit(solution)/shard_map/ppermute | solution.py:30
  17.6 0.7 collective-permute-start.6
  18.6 1.5 %collective-permute-done.5 = f32[2,2,1,3,1,1,256]{6,5,3,0,4,2,1:T(1,128)S(1)} collective-permute-done((f32[2,2,1,3,1,1,256]{6,5,3,0,4,2,1:T(1,128)S(1)}, f32[2,2,1,3,1,1,256]{6,5,3,0,4,2,1:T(1,128)S(1)}, u32[]{:S(2)}, u32[]{:S(2)}) %collective-permute-start.5) | collective-permute-done | bytes 12320 | tf_op jit(solution)/shard_map/ppermute | solution.py:30
  20.0 1.3 %collective-permute-done.6 = f32[2,2,1,3,1,1,256]{6,5,3,0,4,2,1:T(1,128)S(1)} collective-permute-done((f32[2,2,1,3,1,1,256]{6,5,3,0,4,2,1:T(1,128)S(1)}, f32[2,2,1,3,1,1,256]{6,5,3,0,4,2,1:T(1,128)S(1)}, u32[]{:S(2)}, u32[]{:S(2)}) %collective-permute-start.6) | collective-permute-done | bytes 12320 | tf_op jit(solution)/shard_map/ppermute | solution.py:29
  22.5 0.8 collective-permute-start.7
  23.3 1.3 %collective-permute-start.8 = (f32[2,2,1,3,1,1,256]{6,5,3,0,4,2,1:T(1,128)S(1)}, f32[2,2,1,3,1,1,256]{6,5,3,0,4,2,1:T(1,128)S(1)}, u32[]{:S(2)}, u32[]{:S(2)}) collective-permute-start(f32[2,2,1,3,1,1,256]{6,5,3,0,4,2,1:T(1,128)S(1)} %get-tuple-element.574), channel_id=1, source_target_pairs={{0,16},{16,0},{1,17},{17,1},{2,18},{18,2},{3,19},{19,3},{4,20},{20... | collective-permute-start | bytes 36872 | tf_op jit(solution)/shard_map/ppermute | solution.py:29
  24.8 1.5 %collective-permute-done.7 = f32[2,2,1,3,1,1,256]{6,5,3,0,4,2,1:T(1,128)S(1)} collective-permute-done((f32[2,2,1,3,1,1,256]{6,5,3,0,4,2,1:T(1,128)S(1)}, f32[2,2,1,3,1,1,256]{6,5,3,0,4,2,1:T(1,128)S(1)}, u32[]{:S(2)}, u32[]{:S(2)}) %collective-permute-start.7) | collective-permute-done | bytes 12320 | tf_op jit(solution)/shard_map/ppermute | solution.py:30
  26.3 0.7 collective-permute-done.8
  30.8 1.4 %collective-permute-start.10 = (f32[2,2,4,3,1,1,256]{6,2,5,4,3,1,0:T(4,128)S(1)}, f32[2,2,4,3,1,1,256]{6,2,5,4,3,1,0:T(4,128)S(1)}, u32[]{:S(2)}, u32[]{:S(2)}) collective-permute-start(f32[2,2,4,3,1,1,256]{6,2,5,4,3,1,0:T(4,128)S(1)} %get-tuple-element.300), channel_id=1, source_target_pairs={{0,16},{16,0},{1,17},{17,1},{2,18},{18,2},{3,19},{19,3},{4,20},{20... | collective-permute-start | bytes 147464 | tf_op jit(solution)/shard_map/ppermute | solution.py:29
  32.2 0.7 collective-permute-start.9
  33.2 4.4 %collective-permute-start.11 = (f32[2,2,2,3,1,2,256]{6,2,5,4,3,1,0:T(2,128)S(1)}, f32[2,2,2,3,1,2,256]{6,2,5,4,3,1,0:T(2,128)S(1)}, u32[]{:S(2)}, u32[]{:S(2)}) collective-permute-start(f32[2,2,2,3,1,2,256]{6,2,5,4,3,1,0:T(2,128)S(1)} %get-tuple-element.302), channel_id=1, source_target_pairs={{0,15},{1,0},{2,1},{3,2},{4,3},{5,4},{6,5},{7,6},{8,7},{9,8},{10,9... | collective-permute-start | bytes 147464 | tf_op jit(solution)/shard_map/ppermute | solution.py:19
  38.7 0.7 collective-permute-done.11
  42.4 1.4 %collective-permute-start.13 = (f32[2,2,4,3,1,1,256]{6,2,5,4,3,1,0:T(4,128)S(1)}, f32[2,2,4,3,1,1,256]{6,2,5,4,3,1,0:T(4,128)S(1)}, u32[]{:S(2)}, u32[]{:S(2)}) collective-permute-start(f32[2,2,4,3,1,1,256]{6,2,5,4,3,1,0:T(4,128)S(1)} %get-tuple-element.267), channel_id=1, source_target_pairs={{16,0},{0,16},{17,1},{1,17},{18,2},{2,18},{19,3},{3,19},{20,4},{4,... | collective-permute-start | bytes 147464 | tf_op jit(solution)/shard_map/ppermute | solution.py:30
  43.8 0.7 collective-permute-start.14
  44.6 4.0 %collective-permute-start.15 = (f32[2,2,2,3,1,2,256]{6,2,5,4,3,1,0:T(2,128)S(1)}, f32[2,2,2,3,1,2,256]{6,2,5,4,3,1,0:T(2,128)S(1)}, u32[]{:S(2)}, u32[]{:S(2)}) collective-permute-start(f32[2,2,2,3,1,2,256]{6,2,5,4,3,1,0:T(2,128)S(1)} %get-tuple-element.273), channel_id=1, source_target_pairs={{0,15},{1,0},{2,1},{3,2},{4,3},{5,4},{6,5},{7,6},{8,7},{9,8},{10,9... | collective-permute-start | bytes 147464 | tf_op jit(solution)/shard_map/ppermute | solution.py:19
  52.9 2.3 %collective-permute-done.16 = f32[2,2,2,3,1,2,256]{6,2,5,4,3,1,0:T(2,128)S(1)} collective-permute-done((f32[2,2,2,3,1,2,256]{6,2,5,4,3,1,0:T(2,128)S(1)}, f32[2,2,2,3,1,2,256]{6,2,5,4,3,1,0:T(2,128)S(1)}, u32[]{:S(2)}, u32[]{:S(2)}) %collective-permute-start.16) | collective-permute-done | bytes 49184 | tf_op jit(solution)/shard_map/ppermute | solution.py:19
  56.5 1.4 %collective-permute-start.17 = (f32[2,2,4,3,1,1,256]{6,2,5,4,3,1,0:T(4,128)S(1)}, f32[2,2,4,3,1,1,256]{6,2,5,4,3,1,0:T(4,128)S(1)}, u32[]{:S(2)}, u32[]{:S(2)}) collective-permute-start(f32[2,2,4,3,1,1,256]{6,2,5,4,3,1,0:T(4,128)S(1)} %get-tuple-element.229), channel_id=1, source_target_pairs={{16,0},{0,16},{17,1},{1,17},{18,2},{2,18},{19,3},{3,19},{20,4},{4,... | collective-permute-start | bytes 147464 | tf_op jit(solution)/shard_map/ppermute | solution.py:30
  57.9 0.7 collective-permute-start.18
  59.3 4.4 %collective-permute-start.19 = (f32[2,2,2,3,1,2,256]{6,2,5,4,3,1,0:T(2,128)S(1)}, f32[2,2,2,3,1,2,256]{6,2,5,4,3,1,0:T(2,128)S(1)}, u32[]{:S(2)}, u32[]{:S(2)}) collective-permute-start(f32[2,2,2,3,1,2,256]{6,2,5,4,3,1,0:T(2,128)S(1)} %get-tuple-element.236), channel_id=1, source_target_pairs={{0,15},{1,0},{2,1},{3,2},{4,3},{5,4},{6,5},{7,6},{8,7},{9,8},{10,9... | collective-permute-start | bytes 147464 | tf_op jit(solution)/shard_map/ppermute | solution.py:19
  68.6 1.4 %collective-permute-start.21 = (f32[2,2,4,3,1,1,256]{6,2,5,4,3,1,0:T(4,128)S(1)}, f32[2,2,4,3,1,1,256]{6,2,5,4,3,1,0:T(4,128)S(1)}, u32[]{:S(2)}, u32[]{:S(2)}) collective-permute-start(f32[2,2,4,3,1,1,256]{6,2,5,4,3,1,0:T(4,128)S(1)} %get-tuple-element.200), channel_id=1, source_target_pairs={{16,0},{0,16},{17,1},{1,17},{18,2},{2,18},{19,3},{3,19},{20,4},{4,... | collective-permute-start | bytes 147464 | tf_op jit(solution)/shard_map/ppermute | solution.py:30
  70.0 0.7 collective-permute-start.22
  71.4 4.4 %collective-permute-start.23 = (f32[2,2,2,3,1,2,256]{6,2,5,4,3,1,0:T(2,128)S(1)}, f32[2,2,2,3,1,2,256]{6,2,5,4,3,1,0:T(2,128)S(1)}, u32[]{:S(2)}, u32[]{:S(2)}) collective-permute-start(f32[2,2,2,3,1,2,256]{6,2,5,4,3,1,0:T(2,128)S(1)} %get-tuple-element.206), channel_id=1, source_target_pairs={{0,15},{1,0},{2,1},{3,2},{4,3},{5,4},{6,5},{7,6},{8,7},{9,8},{10,9... | collective-permute-start | bytes 147464 | tf_op jit(solution)/shard_map/ppermute | solution.py:19
  79.3 0.7 copy.399
  (509 shorter events, 26.6 us)
Async XLA Ops:
  0.0 0.7 copy-start.3
  0.0 4.8 %copy-start.2 = (f32[4,2,3,3,1,2,256]{6,5,4,3,2,1,0:T(2,128)S(1)}, f32[4,2,3,3,1,2,256]{6,5,4,3,2,1,0:T(2,128)}, u32[]{:S(2)}) copy-start(f32[4,2,3,3,1,2,256]{6,5,4,3,2,1,0:T(2,128)} %param.4) | copy-start | bytes 442372
  1.6 5.4 %copy-start = (f32[2,2,1,3,1,2,256]{6,5,3,1,0,4,2:T(2,128)}, f32[2,2,1,3,1,2,256]{6,5,3,1,0,4,2:T(2,128)S(1)}, u32[]{:S(2)}) copy-start(f32[2,2,1,3,1,2,256]{6,5,3,1,0,4,2:T(2,128)S(1)} %reshape.6794) | copy-start | bytes 73732
  1.7 7.1 %collective-permute-start = (f32[2,2,1,3,1,1,256]{6,5,1,3,0,4,2:T(1,128)S(1)}, f32[2,2,1,3,1,1,256]{6,5,1,3,0,4,2:T(1,128)S(1)}, u32[]{:S(2)}, u32[]{:S(2)}) collective-permute-start(f32[2,2,1,3,1,1,256]{6,5,1,3,0,4,2:T(1,128)S(1)} %get-tuple-element.597), channel_id=1, source_target_pairs={{16,0},{0,16},{17,1},{1,17},{18,2},{2,18},{19,3},{3,19},{20,4},{4,... | collective-permute-start | bytes 36872 | tf_op jit(solution)/shard_map/ppermute | solution.py:30
  4.7 4.1 %collective-permute-start.2 = (f32[2,2,1,3,1,1,256]{6,5,1,3,0,4,2:T(1,128)S(1)}, f32[2,2,1,3,1,1,256]{6,5,1,3,0,4,2:T(1,128)S(1)}, u32[]{:S(2)}, u32[]{:S(2)}) collective-permute-start(f32[2,2,1,3,1,1,256]{6,5,1,3,0,4,2:T(1,128)S(1)} %get-tuple-element.598), channel_id=1, source_target_pairs={{0,16},{16,0},{1,17},{17,1},{2,18},{18,2},{3,19},{19,3},{4,20},{20... | collective-permute-start | bytes 36872 | tf_op jit(solution)/shard_map/ppermute | solution.py:29
  4.8 5.0 %collective-permute-start.1 = (f32[2,3,3,1,1,256]{5,4,2,1,0,3:T(1,128)S(1)}, f32[2,3,3,1,1,256]{5,4,2,1,0,3:T(1,128)S(1)}, u32[]{:S(2)}, u32[]{:S(2)}) collective-permute-start(f32[2,3,3,1,1,256]{5,4,2,1,0,3:T(1,128)S(1)} %get-tuple-element.349), channel_id=1, source_target_pairs={{0,16},{16,0},{1,17},{17,1},{2,18},{18,2},{3,19},{19,3},{4,20},{20... | collective-permute-start | bytes 55304 | tf_op jit(solution)/shard_map/ppermute | solution.py:19
  7.2 0.7 slice-start
  7.9 0.7 copy-start.4
  8.7 0.7 copy-start.1
  10.6 3.8 %collective-permute-start.3 = (f32[2,2,1,3,1,1,256]{6,5,3,0,4,2,1:T(1,128)S(1)}, f32[2,2,1,3,1,1,256]{6,5,3,0,4,2,1:T(1,128)S(1)}, u32[]{:S(2)}, u32[]{:S(2)}) collective-permute-start(f32[2,2,1,3,1,1,256]{6,5,3,0,4,2,1:T(1,128)S(1)} %get-tuple-element.589), channel_id=1, source_target_pairs={{16,0},{0,16},{17,1},{1,17},{18,2},{2,18},{19,3},{3,19},{20,4},{4,... | collective-permute-start | bytes 36872 | tf_op jit(solution)/shard_map/ppermute | solution.py:30
  11.4 3.7 %collective-permute-start.4 = (f32[2,2,1,3,1,1,256]{6,5,3,0,4,2,1:T(1,128)S(1)}, f32[2,2,1,3,1,1,256]{6,5,3,0,4,2,1:T(1,128)S(1)}, u32[]{:S(2)}, u32[]{:S(2)}) collective-permute-start(f32[2,2,1,3,1,1,256]{6,5,3,0,4,2,1:T(1,128)S(1)} %get-tuple-element.590), channel_id=1, source_target_pairs={{0,16},{16,0},{1,17},{17,1},{2,18},{18,2},{3,19},{19,3},{4,20},{20... | collective-permute-start | bytes 36872 | tf_op jit(solution)/shard_map/ppermute | solution.py:29
  16.3 3.8 %collective-permute-start.5 = (f32[2,2,1,3,1,1,256]{6,5,3,0,4,2,1:T(1,128)S(1)}, f32[2,2,1,3,1,1,256]{6,5,3,0,4,2,1:T(1,128)S(1)}, u32[]{:S(2)}, u32[]{:S(2)}) collective-permute-start(f32[2,2,1,3,1,1,256]{6,5,3,0,4,2,1:T(1,128)S(1)} %get-tuple-element.581), channel_id=1, source_target_pairs={{16,0},{0,16},{17,1},{1,17},{18,2},{2,18},{19,3},{3,19},{20,4},{4,... | collective-permute-start | bytes 36872 | tf_op jit(solution)/shard_map/ppermute | solution.py:30
  17.6 3.7 %collective-permute-start.6 = (f32[2,2,1,3,1,1,256]{6,5,3,0,4,2,1:T(1,128)S(1)}, f32[2,2,1,3,1,1,256]{6,5,3,0,4,2,1:T(1,128)S(1)}, u32[]{:S(2)}, u32[]{:S(2)}) collective-permute-start(f32[2,2,1,3,1,1,256]{6,5,3,0,4,2,1:T(1,128)S(1)} %get-tuple-element.582), channel_id=1, source_target_pairs={{0,16},{16,0},{1,17},{17,1},{2,18},{18,2},{3,19},{19,3},{4,20},{20... | collective-permute-start | bytes 36872 | tf_op jit(solution)/shard_map/ppermute | solution.py:29
  22.5 3.8 %collective-permute-start.7 = (f32[2,2,1,3,1,1,256]{6,5,3,0,4,2,1:T(1,128)S(1)}, f32[2,2,1,3,1,1,256]{6,5,3,0,4,2,1:T(1,128)S(1)}, u32[]{:S(2)}, u32[]{:S(2)}) collective-permute-start(f32[2,2,1,3,1,1,256]{6,5,3,0,4,2,1:T(1,128)S(1)} %get-tuple-element.573), channel_id=1, source_target_pairs={{16,0},{0,16},{17,1},{1,17},{18,2},{2,18},{19,3},{3,19},{20,4},{4,... | collective-permute-start | bytes 36872 | tf_op jit(solution)/shard_map/ppermute | solution.py:30
  23.3 3.7 %collective-permute-start.8 = (f32[2,2,1,3,1,1,256]{6,5,3,0,4,2,1:T(1,128)S(1)}, f32[2,2,1,3,1,1,256]{6,5,3,0,4,2,1:T(1,128)S(1)}, u32[]{:S(2)}, u32[]{:S(2)}) collective-permute-start(f32[2,2,1,3,1,1,256]{6,5,3,0,4,2,1:T(1,128)S(1)} %get-tuple-element.574), channel_id=1, source_target_pairs={{0,16},{16,0},{1,17},{17,1},{2,18},{18,2},{3,19},{19,3},{4,20},{20... | collective-permute-start | bytes 36872 | tf_op jit(solution)/shard_map/ppermute | solution.py:29
  30.8 7.1 %collective-permute-start.10 = (f32[2,2,4,3,1,1,256]{6,2,5,4,3,1,0:T(4,128)S(1)}, f32[2,2,4,3,1,1,256]{6,2,5,4,3,1,0:T(4,128)S(1)}, u32[]{:S(2)}, u32[]{:S(2)}) collective-permute-start(f32[2,2,4,3,1,1,256]{6,2,5,4,3,1,0:T(4,128)S(1)} %get-tuple-element.300), channel_id=1, source_target_pairs={{0,16},{16,0},{1,17},{17,1},{2,18},{18,2},{3,19},{19,3},{4,20},{20... | collective-permute-start | bytes 147464 | tf_op jit(solution)/shard_map/ppermute | solution.py:29
  32.2 5.7 %collective-permute-start.9 = (f32[2,2,4,3,1,1,256]{6,2,5,4,3,1,0:T(4,128)S(1)}, f32[2,2,4,3,1,1,256]{6,2,5,4,3,1,0:T(4,128)S(1)}, u32[]{:S(2)}, u32[]{:S(2)}) collective-permute-start(f32[2,2,4,3,1,1,256]{6,2,5,4,3,1,0:T(4,128)S(1)} %get-tuple-element.299), channel_id=1, source_target_pairs={{16,0},{0,16},{17,1},{1,17},{18,2},{2,18},{19,3},{3,19},{20,4},{4,... | collective-permute-start | bytes 147464 | tf_op jit(solution)/shard_map/ppermute | solution.py:30
  33.2 7.4 %collective-permute-start.12 = (f32[2,2,2,3,1,2,256]{6,2,5,4,3,1,0:T(2,128)S(1)}, f32[2,2,2,3,1,2,256]{6,2,5,4,3,1,0:T(2,128)S(1)}, u32[]{:S(2)}, u32[]{:S(2)}) collective-permute-start(f32[2,2,2,3,1,2,256]{6,2,5,4,3,1,0:T(2,128)S(1)} %pad_maximum_fusion.42), channel_id=1, source_target_pairs={{0,1},{1,2},{2,3},{3,4},{4,5},{5,6},{6,7},{7,8},{8,9},{9,10},{10,1... | collective-permute-start | bytes 147464 | tf_op jit(solution)/shard_map/ppermute | solution.py:19
  33.2 6.2 %collective-permute-start.11 = (f32[2,2,2,3,1,2,256]{6,2,5,4,3,1,0:T(2,128)S(1)}, f32[2,2,2,3,1,2,256]{6,2,5,4,3,1,0:T(2,128)S(1)}, u32[]{:S(2)}, u32[]{:S(2)}) collective-permute-start(f32[2,2,2,3,1,2,256]{6,2,5,4,3,1,0:T(2,128)S(1)} %get-tuple-element.302), channel_id=1, source_target_pairs={{0,15},{1,0},{2,1},{3,2},{4,3},{5,4},{6,5},{7,6},{8,7},{9,8},{10,9... | collective-permute-start | bytes 147464 | tf_op jit(solution)/shard_map/ppermute | solution.py:19
  42.4 6.9 %collective-permute-start.13 = (f32[2,2,4,3,1,1,256]{6,2,5,4,3,1,0:T(4,128)S(1)}, f32[2,2,4,3,1,1,256]{6,2,5,4,3,1,0:T(4,128)S(1)}, u32[]{:S(2)}, u32[]{:S(2)}) collective-permute-start(f32[2,2,4,3,1,1,256]{6,2,5,4,3,1,0:T(4,128)S(1)} %get-tuple-element.267), channel_id=1, source_target_pairs={{16,0},{0,16},{17,1},{1,17},{18,2},{2,18},{19,3},{3,19},{20,4},{4,... | collective-permute-start | bytes 147464 | tf_op jit(solution)/shard_map/ppermute | solution.py:30
  43.8 5.5 %collective-permute-start.14 = (f32[2,2,4,3,1,1,256]{6,2,5,4,3,1,0:T(4,128)S(1)}, f32[2,2,4,3,1,1,256]{6,2,5,4,3,1,0:T(4,128)S(1)}, u32[]{:S(2)}, u32[]{:S(2)}) collective-permute-start(f32[2,2,4,3,1,1,256]{6,2,5,4,3,1,0:T(4,128)S(1)} %get-tuple-element.268), channel_id=1, source_target_pairs={{0,16},{16,0},{1,17},{17,1},{2,18},{18,2},{3,19},{19,3},{4,20},{20... | collective-permute-start | bytes 147464 | tf_op jit(solution)/shard_map/ppermute | solution.py:29
  44.6 7.5 %collective-permute-start.15 = (f32[2,2,2,3,1,2,256]{6,2,5,4,3,1,0:T(2,128)S(1)}, f32[2,2,2,3,1,2,256]{6,2,5,4,3,1,0:T(2,128)S(1)}, u32[]{:S(2)}, u32[]{:S(2)}) collective-permute-start(f32[2,2,2,3,1,2,256]{6,2,5,4,3,1,0:T(2,128)S(1)} %get-tuple-element.273), channel_id=1, source_target_pairs={{0,15},{1,0},{2,1},{3,2},{4,3},{5,4},{6,5},{7,6},{8,7},{9,8},{10,9... | collective-permute-start | bytes 147464 | tf_op jit(solution)/shard_map/ppermute | solution.py:19
  48.8 6.4 %collective-permute-start.16 = (f32[2,2,2,3,1,2,256]{6,2,5,4,3,1,0:T(2,128)S(1)}, f32[2,2,2,3,1,2,256]{6,2,5,4,3,1,0:T(2,128)S(1)}, u32[]{:S(2)}, u32[]{:S(2)}) collective-permute-start(f32[2,2,2,3,1,2,256]{6,2,5,4,3,1,0:T(2,128)S(1)} %pad_maximum_fusion.43), channel_id=1, source_target_pairs={{0,1},{1,2},{2,3},{3,4},{4,5},{5,6},{6,7},{7,8},{8,9},{9,10},{10,1... | collective-permute-start | bytes 147464 | tf_op jit(solution)/shard_map/ppermute | solution.py:19
  56.5 7.4 %collective-permute-start.17 = (f32[2,2,4,3,1,1,256]{6,2,5,4,3,1,0:T(4,128)S(1)}, f32[2,2,4,3,1,1,256]{6,2,5,4,3,1,0:T(4,128)S(1)}, u32[]{:S(2)}, u32[]{:S(2)}) collective-permute-start(f32[2,2,4,3,1,1,256]{6,2,5,4,3,1,0:T(4,128)S(1)} %get-tuple-element.229), channel_id=1, source_target_pairs={{16,0},{0,16},{17,1},{1,17},{18,2},{2,18},{19,3},{3,19},{20,4},{4,... | collective-permute-start | bytes 147464 | tf_op jit(solution)/shard_map/ppermute | solution.py:30
  57.9 6.0 %collective-permute-start.18 = (f32[2,2,4,3,1,1,256]{6,2,5,4,3,1,0:T(4,128)S(1)}, f32[2,2,4,3,1,1,256]{6,2,5,4,3,1,0:T(4,128)S(1)}, u32[]{:S(2)}, u32[]{:S(2)}) collective-permute-start(f32[2,2,4,3,1,1,256]{6,2,5,4,3,1,0:T(4,128)S(1)} %get-tuple-element.230), channel_id=1, source_target_pairs={{0,16},{16,0},{1,17},{17,1},{2,18},{18,2},{3,19},{19,3},{4,20},{20... | collective-permute-start | bytes 147464 | tf_op jit(solution)/shard_map/ppermute | solution.py:29
  59.3 8.0 %collective-permute-start.20 = (f32[2,2,2,3,1,2,256]{6,2,5,4,3,1,0:T(2,128)S(1)}, f32[2,2,2,3,1,2,256]{6,2,5,4,3,1,0:T(2,128)S(1)}, u32[]{:S(2)}, u32[]{:S(2)}) collective-permute-start(f32[2,2,2,3,1,2,256]{6,2,5,4,3,1,0:T(2,128)S(1)} %pad_maximum_fusion.44), channel_id=1, source_target_pairs={{0,1},{1,2},{2,3},{3,4},{4,5},{5,6},{6,7},{7,8},{8,9},{9,10},{10,1... | collective-permute-start | bytes 147464 | tf_op jit(solution)/shard_map/ppermute | solution.py:19
  59.3 7.4 %collective-permute-start.19 = (f32[2,2,2,3,1,2,256]{6,2,5,4,3,1,0:T(2,128)S(1)}, f32[2,2,2,3,1,2,256]{6,2,5,4,3,1,0:T(2,128)S(1)}, u32[]{:S(2)}, u32[]{:S(2)}) collective-permute-start(f32[2,2,2,3,1,2,256]{6,2,5,4,3,1,0:T(2,128)S(1)} %get-tuple-element.236), channel_id=1, source_target_pairs={{0,15},{1,0},{2,1},{3,2},{4,3},{5,4},{6,5},{7,6},{8,7},{9,8},{10,9... | collective-permute-start | bytes 147464 | tf_op jit(solution)/shard_map/ppermute | solution.py:19
  68.6 7.5 %collective-permute-start.21 = (f32[2,2,4,3,1,1,256]{6,2,5,4,3,1,0:T(4,128)S(1)}, f32[2,2,4,3,1,1,256]{6,2,5,4,3,1,0:T(4,128)S(1)}, u32[]{:S(2)}, u32[]{:S(2)}) collective-permute-start(f32[2,2,4,3,1,1,256]{6,2,5,4,3,1,0:T(4,128)S(1)} %get-tuple-element.200), channel_id=1, source_target_pairs={{16,0},{0,16},{17,1},{1,17},{18,2},{2,18},{19,3},{3,19},{20,4},{4,... | collective-permute-start | bytes 147464 | tf_op jit(solution)/shard_map/ppermute | solution.py:30
  70.0 6.1 %collective-permute-start.22 = (f32[2,2,4,3,1,1,256]{6,2,5,4,3,1,0:T(4,128)S(1)}, f32[2,2,4,3,1,1,256]{6,2,5,4,3,1,0:T(4,128)S(1)}, u32[]{:S(2)}, u32[]{:S(2)}) collective-permute-start(f32[2,2,4,3,1,1,256]{6,2,5,4,3,1,0:T(4,128)S(1)} %get-tuple-element.199), channel_id=1, source_target_pairs={{0,16},{16,0},{1,17},{17,1},{2,18},{18,2},{3,19},{19,3},{4,20},{20... | collective-permute-start | bytes 147464 | tf_op jit(solution)/shard_map/ppermute | solution.py:29
  71.3 7.8 %collective-permute-start.24 = (f32[2,2,2,3,1,2,256]{6,2,5,4,3,1,0:T(2,128)S(1)}, f32[2,2,2,3,1,2,256]{6,2,5,4,3,1,0:T(2,128)S(1)}, u32[]{:S(2)}, u32[]{:S(2)}) collective-permute-start(f32[2,2,2,3,1,2,256]{6,2,5,4,3,1,0:T(2,128)S(1)} %pad_maximum_fusion.45), channel_id=1, source_target_pairs={{0,1},{1,2},{2,3},{3,4},{4,5},{5,6},{6,7},{7,8},{8,9},{9,10},{10,1... | collective-permute-start | bytes 147464 | tf_op jit(solution)/shard_map/ppermute | solution.py:19
  71.4 6.8 %collective-permute-start.23 = (f32[2,2,2,3,1,2,256]{6,2,5,4,3,1,0:T(2,128)S(1)}, f32[2,2,2,3,1,2,256]{6,2,5,4,3,1,0:T(2,128)S(1)}, u32[]{:S(2)}, u32[]{:S(2)}) collective-permute-start(f32[2,2,2,3,1,2,256]{6,2,5,4,3,1,0:T(2,128)S(1)} %get-tuple-element.206), channel_id=1, source_target_pairs={{0,15},{1,0},{2,1},{3,2},{4,3},{5,4},{6,5},{7,6},{8,7},{9,8},{10,9... | collective-permute-start | bytes 147464 | tf_op jit(solution)/shard_map/ppermute | solution.py:19
where the time goes:
time: 80.3 us; the launch traced here: 80 us
  starting transfers between devices  37.4 us (47%)
  other arithmetic  20.3 us (25%)
  waiting for transfers between devices  10.2 us (13%)
  local copies, waits for them, and re-layouts  7.92 us (10%)
  between operations  3.29 us (4%)
  matrix products  0.91 us (1%)
    ppermute x9, starting transfers between devices, passed_along(): lax.ppermute(array, axis, [(i, (i + by) % size) for i in range(size)])  19.7 us
    ppermute x8, starting transfers between devices, extended(): after = lax.ppermute(first, axis, down)  10.8 us
    ppermute x8, starting transfers between devices, extended(): before = lax.ppermute(last, axis, up)  6.94 us
    reduce_sum x46, other arithmetic, colour_times(): out_re = jnp.sum(link_re * field_re - link_im * field_im, axis=3)  5.23 us
    ppermute x8, waiting for transfers between devices, extended(): after = lax.ppermute(first, axis, down)  4.4 us
    another operation x41, other arithmetic, colour_times(): return jnp.stack([out_re, out_im], 1)  3.24 us
    ppermute x9, waiting for transfers between devices, passed_along(): lax.ppermute(array, axis, [(i, (i + by) % size) for i in range(size)])  3.04 us
    ppermute x8, waiting for transfers between devices, extended(): before = lax.ppermute(last, axis, up)  2.78 us
  transfers between devices with their start and end apart: 25, of which 8 were waited for; matrix products, arithmetic and copies ran while one was open for 18% of the time, Pallas kernels for 0%

commit v1 on v0

v1 whole, which is shorter than its diff:
```python
import functools

import jax
import jax.numpy as jnp
from jax import lax
from jax.experimental import pallas as pl
from jax.experimental.pallas import tpu as pltpu
from jax.sharding import PartitionSpec as P

LXY = 16
LANES = 128
N_SMEAR = 4
ITERS = 4

smear_weight = 0.2
hop_kappa = 0.125
gamma_perm = ((3, 2, 1, 0), (3, 2, 1, 0), (2, 3, 0, 1), (2, 3, 0, 1))
gamma_phase = ((1, 1, 3, 3), (2, 0, 0, 2), (1, 3, 3, 1), (0, 0, 0, 0))


def phase_times(code, real, imag):
    if code == 0:
        return (real, imag)
    if code == 1:
        return (-imag, real)
    if code == 2:
        return (-real, -imag)
    return (imag, -real)


def project(hop_dir, sign, psi):
    re, im = psi
    rows_re, rows_im = [], []
    for spin in range(2):
        other = gamma_perm[hop_dir][spin]
        p_re, p_im = phase_times(gamma_phase[hop_dir][spin], re[other], im[other])
        if sign > 0:
            rows_re.append(re[spin] + p_re)
            rows_im.append(im[spin] + p_im)
        else:
            rows_re.append(re[spin] - p_re)
            rows_im.append(im[spin] - p_im)
    return jnp.stack(rows_re), jnp.stack(rows_im)


def add_rows(hop_dir, sign, total, half):
    t_re, t_im = list(total[0]), list(total[1])
    h_re, h_im = half
    for spin in range(2):
        t_re[spin] = t_re[spin] + h_re[spin]
        t_im[spin] = t_im[spin] + h_im[spin]
    for spin in (2, 3):
        other = gamma_perm[hop_dir][spin]
        p_re, p_im = phase_times(gamma_phase[hop_dir][spin], h_re[other], h_im[other])
        if sign > 0:
            t_re[spin] = t_re[spin] + p_re
            t_im[spin] = t_im[spin] + p_im
        else:
            t_re[spin] = t_re[spin] - p_re
            t_im[spin] = t_im[spin] - p_im
    return t_re, t_im


def times_link(links, half, adjoint):
    h_re, h_im = half
    out_re = out_im = None
    for b in range(3):
        if adjoint:
            u_re = links[0, b][None]
            u_im = -links[1, b][None]
        else:
            u_re = jnp.stack([links[0, a, b] for a in range(3)])[None]
            u_im = jnp.stack([links[1, a, b] for a in range(3)])[None]
        b_re = h_re[:, b][:, None]
        b_im = h_im[:, b][:, None]
        t_re = u_re * b_re - u_im * b_im
        t_im = u_re * b_im + u_im * b_re
        out_re = t_re if out_re is None else out_re + t_re
        out_im = t_im if out_im is None else out_im + t_im
    return out_re, out_im


def kernel(
    groups, sheets, thick, amp_ref, site_ref, weight_ref, gauge_ref, out_ref,
    recv, links, send_t, recv_t, stage, src,
    own_sem, g_send, g_recv, t_send, t_recv, f_send, f_recv,
):
    nz = groups * thick
    rows = 2 * nz
    group = lax.axis_index("grp")
    sheet = lax.axis_index("lat")
    ahead = lax.rem(sheet + 1, sheets)
    behind = lax.rem(sheet + sheets - 1, sheets)
    parts = ((0, 54), (54, 18))

    own = [
        pltpu.make_async_copy(
            gauge_ref.at[pl.ds(lo, n)], recv.at[group, pl.ds(lo, n)], own_sem.at[i]
        )
        for i, (lo, n) in enumerate(parts)
    ]
    for copy in own:
        copy.start()

    barrier = pltpu.get_barrier_semaphore()
    for k in range(1, groups):
        pl.semaphore_signal(barrier, inc=1, device_id={"grp": lax.rem(group + k, groups)})
    pl.semaphore_signal(barrier, inc=1, device_id={"lat": ahead})
    pl.semaphore_signal(barrier, inc=1, device_id={"lat": behind})
    pl.semaphore_wait(barrier, groups + 1)

    def gauge_copy(part, k, slot):
        lo, n = parts[part]
        return pltpu.make_async_remote_copy(
            src_ref=gauge_ref.at[pl.ds(lo, n)],
            dst_ref=recv.at[slot, pl.ds(lo, n)],
            send_sem=g_send.at[part, k],
            recv_sem=g_recv.at[part, k],
            device_id={"grp": lax.rem(group + k, groups)},
        )

    for part in range(2):
        for k in range(1, groups):
            gauge_copy(part, k, group).start()

    row = lax.broadcasted_iota(jnp.int32, (rows, LANES), 0)
    lane = lax.broadcasted_iota(jnp.int32, (rows, LANES), 1)
    upper_half = row >= nz
    z = jnp.where(upper_half, row - nz, row)
    col = lane % LXY

    def shifted(field, hop_dir, offset):
        lanes_axis, rows_axis = field.ndim - 1, field.ndim - 2
        if hop_dir == 0:
            if offset > 0:
                return jnp.where(
                    col == LXY - 1,
                    pltpu.roll(field, LXY - 1, lanes_axis),
                    pltpu.roll(field, LANES - 1, lanes_axis),
                )
            return jnp.where(
                col == 0,
                pltpu.roll(field, LANES - LXY + 1, lanes_axis),
                pltpu.roll(field, 1, lanes_axis),
            )
        if hop_dir == 1:
            if offset > 0:
                rolled = pltpu.roll(field, LANES - LXY, lanes_axis)
                edge = lane >= LANES - LXY
            else:
                rolled = pltpu.roll(field, LXY, lanes_axis)
                edge = lane < LXY
            return jnp.where(edge, pltpu.roll(rolled, nz, rows_axis), rolled)
        if offset > 0:
            return jnp.where(
                z == nz - 1,
                pltpu.roll(field, nz - 1, rows_axis),
                pltpu.roll(field, rows - 1, rows_axis),
            )
        return jnp.where(
            z == 0,
            pltpu.roll(field, rows - nz + 1, rows_axis),
            pltpu.roll(field, 1, rows_axis),
        )

    def shifted_pair(pair, hop_dir, offset):
        return shifted(pair[0], hop_dir, offset), shifted(pair[1], hop_dir, offset)

    cells = z * (2 * LANES) + jnp.where(upper_half, LANES, 0) + lane
    points = site_ref.shape[2]

    def add_point(p, fields):
        hit = cells == site_ref[group, 0, p]
        return tuple(
            fields[i] + jnp.where(hit, amp_ref[group, i // 3, i % 3, 0, p], 0.0)
            for i in range(6)
        )

    zero = jnp.zeros((rows, LANES), jnp.float32)
    fields = lax.fori_loop(0, points, add_point, (zero,) * 6)
    colour = (jnp.stack(fields[:3])[None], jnp.stack(fields[3:])[None])

    def arrange(part):
        lo, n = parts[part]
        own[part].wait()
        for k in range(1, groups):
            gauge_copy(part, k, lax.rem(group + groups - k, groups)).wait_recv()
        for owner in range(groups):
            for half in range(2):
                to = half * nz + owner * thick
                links[pl.ds(lo, n), to : to + thick, :] = recv[
                    owner, pl.ds(lo, n), half * thick : (half + 1) * thick, :
                ]

    def link(hop_dir):
        class View:
            def __getitem__(self, index):
                base = hop_dir * 18 + index[0] * 9 + index[1] * 3
                if len(index) == 3:
                    return links[base + index[2]]
                return links[base : base + 3]

        return View()

    arrange(0)
    norm = 1.0 + 6.0 * smear_weight

    def smear(_, colour):
        total = None
        for hop_dir in range(3):
            fwd = times_link(link(hop_dir), shifted_pair(colour, hop_dir, 1), False)
            back = shifted_pair(times_link(link(hop_dir), colour, True), hop_dir, -1)
            add = (fwd[0] + back[0], fwd[1] + back[1])
            total = add if total is None else (total[0] + add[0], total[1] + add[1])
        return tuple(
            (1.0 / norm) * colour[i] + (smear_weight / norm) * total[i] for i in range(2)
        )

    colour = lax.fori_loop(0, N_SMEAR, smear, colour)
    c_re, c_im = colour[0][0], colour[1][0]
    for spin in range(4):
        w_re = weight_ref[group, 0, spin]
        w_im = weight_ref[group, 1, spin]
        src[0, spin] = w_re * c_re - w_im * c_im
        src[1, spin] = w_re * c_im + w_im * c_re

    arrange(1)
    sign_low = jnp.where(sheet == 0, -1.0, 1.0).astype(jnp.float32)
    sign_high = jnp.where(sheet == sheets - 1, -1.0, 1.0).astype(jnp.float32)

    def t_copy(step, way):
        return pltpu.make_async_remote_copy(
            src_ref=send_t.at[step, way],
            dst_ref=recv_t.at[step, way],
            send_sem=t_send.at[step, way],
            recv_sem=t_recv.at[step, way],
            device_id={"lat": behind if way == 0 else ahead},
        )

    def hop(step, psi):
        psi = (psi[0], psi[1])
        minus = project(3, -1, psi)
        send_t[step, 0, 0] = minus[0]
        send_t[step, 0, 1] = minus[1]
        t_copy(step, 0).start()
        plus = times_link(link(3), project(3, 1, psi), True)
        send_t[step, 1, 0] = plus[0]
        send_t[step, 1, 1] = plus[1]
        t_copy(step, 1).start()
        zeros = jnp.zeros((3, rows, LANES), jnp.float32)
        total = ([zeros] * 4, [zeros] * 4)
        for hop_dir in range(3):
            half = shifted_pair(project(hop_dir, -1, psi), hop_dir, 1)
            total = add_rows(hop_dir, -1, total, times_link(link(hop_dir), half, False))
            half = times_link(link(hop_dir), project(hop_dir, 1, psi), True)
            total = add_rows(hop_dir, 1, total, shifted_pair(half, hop_dir, -1))
        t_copy(step, 0).wait_recv()
        half = (sign_high * recv_t[step, 0, 0], sign_high * recv_t[step, 0, 1])
        total = add_rows(3, -1, total, times_link(link(3), half, False))
        t_copy(step, 1).wait_recv()
        half = (sign_low * recv_t[step, 1, 0], sign_low * recv_t[step, 1, 1])
        total = add_rows(3, 1, total, half)
        return tuple(src[i] + hop_kappa * jnp.stack(total[i]) for i in range(2))

    psi = lax.fori_loop(0, ITERS, hop, (src[0], src[1]))

    for owner in range(groups):
        for half in range(2):
            at = half * nz + owner * thick
            for i in range(2):
                stage[owner, i, :, :, half * thick : (half + 1) * thick, :] = psi[i][
                    :, :, at : at + thick, :
                ]

    def final_copy(k, slot, to):
        return pltpu.make_async_remote_copy(
            src_ref=stage.at[slot],
            dst_ref=out_ref.at[to],
            send_sem=f_send.at[k],
            recv_sem=f_recv.at[k],
            device_id={"grp": lax.rem(group + k, groups)},
        )

    for k in range(1, groups):
        final_copy(k, lax.rem(group + k, groups), group).start()
    mine = pltpu.make_async_copy(stage.at[group], out_ref.at[group], own_sem.at[2])
    mine.start()

    for part in range(2):
        for k in range(1, groups):
            gauge_copy(part, k, group).wait_send()
    for step in range(ITERS):
        for way in range(2):
            t_copy(step, way).wait_send()
    mine.wait()
    for k in range(1, groups):
        final_copy(k, lax.rem(group + k, groups), group).wait_send()
        final_copy(k, group, lax.rem(group + groups - k, groups)).wait_recv()


def on_device(gauge, amplitudes, source_sites, spin_weights):
    groups = lax.axis_size("grp")
    sheets = lax.axis_size("lat")
    thick = gauge.shape[5]
    plane = gauge.shape[6]
    sides = amplitudes.shape[0]
    assert sides == groups and gauge.shape[4] == 1 and plane == 2 * LANES
    rows = 2 * thick * groups
    blocks = jnp.swapaxes(gauge.reshape(72, thick, 2, LANES), 1, 2).reshape(72, 2 * thick, LANES)
    smem = pl.BlockSpec(memory_space=pltpu.SMEM)
    out = pl.pallas_call(
        functools.partial(kernel, groups, sheets, thick),
        out_shape=jax.ShapeDtypeStruct((sides, 2, 4, 3, 2 * thick, LANES), jnp.float32),
        in_specs=[smem, smem, smem, pl.BlockSpec(memory_space=pl.ANY)],
        out_specs=pl.BlockSpec(memory_space=pl.ANY),
        scratch_shapes=[
            pltpu.VMEM((groups, 72, 2 * thick, LANES), jnp.float32),
            pltpu.VMEM((72, rows, LANES), jnp.float32),
            pltpu.VMEM((ITERS, 2, 2, 2, 3, rows, LANES), jnp.float32),
            pltpu.VMEM((ITERS, 2, 2, 2, 3, rows, LANES), jnp.float32),
            pltpu.VMEM((groups, 2, 4, 3, 2 * thick, LANES), jnp.float32),
            pltpu.VMEM((2, 4, 3, rows, LANES), jnp.float32),
            pltpu.SemaphoreType.DMA((3,)),
            pltpu.SemaphoreType.DMA((2, groups)),
            pltpu.SemaphoreType.DMA((2, groups)),
            pltpu.SemaphoreType.DMA((ITERS, 2)),
            pltpu.SemaphoreType.DMA((ITERS, 2)),
            pltpu.SemaphoreType.DMA((groups,)),
            pltpu.SemaphoreType.DMA((groups,)),
        ],
        compiler_params=pltpu.CompilerParams(
            collective_id=0, has_side_effects=True, vmem_limit_bytes=32 * 1024 * 1024
        ),
    )(amplitudes, source_sites, spin_weights, blocks)
    out = jnp.swapaxes(out.reshape(sides, 2, 4, 3, 2, thick, LANES), 4, 5)
    return out.reshape(sides, 2, 4, 3, 1, thick, plane)


def solution(mesh):
    placed = (
        P(None, None, None, None, "lat", "grp", None),
        P(None, None, None, "lat", None),
        P(None, "lat", None),
        P(),
    )
    return jax.shard_map(
        on_device,
        mesh=mesh,
        in_specs=placed,
        out_specs=P(None, None, None, None, "lat", "grp", None),
        check_vma=False,
    )
```

time: 80.3 us -> 34 us (0.42)
  starting transfers between devices: 37.4 us -> 0 us
  Pallas kernels: 0 us -> 30.2 us
  other arithmetic: 20.3 us -> 0 us
  waiting for transfers between devices: 10.2 us -> 0 us
  local copies, waits for them, and re-layouts: 7.92 us -> 3.6 us
  between operations: 3.29 us -> 0.01 us
  matrix products: 0.91 us -> 0 us
    ppermute x25 -> x0, starting transfers between devices: 37.4 us -> none  [the longest x9 19.7 us: passed_along(): lax.ppermute(array, axis, [(i, (i + by) % size) for i in range(size)])]
    pallas_call x0 -> x1, Pallas kernels: none -> 30.2 us  [on_device(): pl.pallas_call(functools.partial(kernel, groups, sheets, thick), out_shap...]
    ppermute x25 -> x0, waiting for transfers between devices: 10.2 us -> none  [the longest x8 4.4 us: extended(): after = lax.ppermute(first, axis, down)]
    another operation x98 -> x0, other arithmetic: 5.44 us -> none  [the longest x41 3.24 us: colour_times(): return jnp.stack([out_re, out_im], 1)]
    reduce_sum x46 -> x0, other arithmetic: 5.23 us -> none  [colour_times(): out_re = jnp.sum(link_re * field_re - link_im * field_im, axis=3)]
    slice x58 -> x0, local copies, waits for them, and re-layouts: 2.8 us -> none  [the longest x15 1.39 us: roll_site(): return jnp.roll(field, offset * LXY, axis=-1)]
    add x13 -> x0, other arithmetic: 1.97 us -> none  [the longest x4 0.74 us: on_device(): spinor = source + hop_kappa * total]
    select_n x12 -> x0, other arithmetic: 1.92 us -> none  [the longest x8 1.03 us: roll_site(): jnp.where(column == LXY - 1, jnp.roll(field, LXY - 1, axis=-1), jnp.roll(...]
  transfers between devices with their start and end apart: 25 -> 0, of which waited for: 8 -> 0; matrix products, arithmetic and copies ran while one was open for 18% -> 0% of each run, Pallas kernels for 0% -> 0%
where the time goes in v1:
time: 34 us; the launch traced here: 33.8 us
  Pallas kernels  30.2 us (89%)
  local copies, waits for them, and re-layouts  3.6 us (11%)
    pallas_call x1, Pallas kernels, on_device(): pl.pallas_call(functools.partial(kernel, groups, sheets, thick), out_shap...  30.2 us
    unnamed x9, local copies, waits for them, and re-layouts  3.6 us

profile of v1, /device:TPU:0, one launch (start us, length us, event | category | flops | bytes accessed | tf_op | source)
XLA Modules:
  0.0 33.8 jit_solution(3260756118552884716)
XLA Ops:
  0.0 0.0 copy-start.3
  0.0 0.7 %copy-done.3 = s32[2,1,32]{2,1,0:T(1,128)S(1)} copy-done((s32[2,1,32]{2,1,0:T(1,128)S(1)}, s32[2,1,32]{2,1,0:T(1,128)}, u32[]{:S(2)}) %copy-start.3) | copy-done | bytes 280
  0.7 0.0 copy-start
  0.7 0.9 %copy-done = f32[4,2,3,3,1,2,256]{6,5,4,3,2,1,0:T(2,128)S(1)} copy-done((f32[4,2,3,3,1,2,256]{6,5,4,3,2,1,0:T(2,128)S(1)}, f32[4,2,3,3,1,2,256]{6,5,4,3,2,1,0:T(2,128)}, u32[]{:S(2)}) %copy-start) | copy-done | bytes 147480
  1.6 0.0 copy-start.1
  1.6 0.7 %copy-done.1 = f32[2,2,3,1,32]{4,3,2,1,0:T(1,128)S(1)} copy-done((f32[2,2,3,1,32]{4,3,2,1,0:T(1,128)S(1)}, f32[2,2,3,1,32]{4,3,2,1,0:T(1,128)}, u32[]{:S(2)}) %copy-start.1) | copy-done | bytes 1560
  2.3 0.0 copy-start.2
  2.3 0.7 %copy-done.2 = f32[2,2,4]{2,1,0:T(2,128)S(1)} copy-done((f32[2,2,4]{2,1,0:T(2,128)S(1)}, f32[2,2,4]{2,1,0:T(2,128)}, u32[]{:S(2)}) %copy-start.2) | copy-done | bytes 88
  3.0 30.2 %shard_map.46 = f32[2,2,4,3,4,128]{5,4,3,2,1,0:T(4,128)S(1)} custom-call(f32[2,2,3,1,32]{4,3,2,1,0:T(1,128)S(1)} %copy-done.1, s32[2,1,32]{2,1,0:T(1,128)S(1)} %copy-done.3, f32[2,2,4]{2,1,0:T(2,128)S(1)} %copy-done.2, f32[72,4,128]{2,1,0:T(4,128)S(1)} %bitcast.11), custom_call_target="tpu_custom_call" | custom-call | tf_op jit(solution)/shard_map/pallas_call | solution.py:311
  33.2 0.6 %copy.8 = f32[2,2,4,3,1,2,256]{6,5,4,3,2,1,0:T(2,128)} copy(f32[2,2,4,3,1,2,256]{6,5,4,3,2,1,0:T(2,128)S(1)} %bitcast.10) | data formatting | bytes 196608
Async XLA Ops:
  0.0 0.7 %copy-start.3 = (s32[2,1,32]{2,1,0:T(1,128)S(1)}, s32[2,1,32]{2,1,0:T(1,128)}, u32[]{:S(2)}) copy-start(s32[2,1,32]{2,1,0:T(1,128)} %site_ref.1) | copy-start | bytes 772
  0.7 0.9 %copy-start = (f32[4,2,3,3,1,2,256]{6,5,4,3,2,1,0:T(2,128)S(1)}, f32[4,2,3,3,1,2,256]{6,5,4,3,2,1,0:T(2,128)}, u32[]{:S(2)}) copy-start(f32[4,2,3,3,1,2,256]{6,5,4,3,2,1,0:T(2,128)} %param.4) | copy-start | bytes 442372
  1.6 0.7 %copy-start.1 = (f32[2,2,3,1,32]{4,3,2,1,0:T(1,128)S(1)}, f32[2,2,3,1,32]{4,3,2,1,0:T(1,128)}, u32[]{:S(2)}) copy-start(f32[2,2,3,1,32]{4,3,2,1,0:T(1,128)} %amp_ref.1) | copy-start | bytes 4612
  2.3 0.7 %copy-start.2 = (f32[2,2,4]{2,1,0:T(2,128)S(1)}, f32[2,2,4]{2,1,0:T(2,128)}, u32[]{:S(2)}) copy-start(f32[2,2,4]{2,1,0:T(2,128)} %weight_ref.1) | copy-start | bytes 196

commit v2 on v1

--- a/solution.py
+++ b/solution.py
@@ -81,9 +81,9 @@
 
 
 def kernel(
-    groups, sheets, thick, amp_ref, site_ref, weight_ref, gauge_ref, out_ref,
-    recv, links, send_t, recv_t, stage, src,
-    own_sem, g_send, g_recv, t_send, t_recv, f_send, f_recv,
+    groups, sheets, thick, amp_hbm, site_hbm, weight_hbm, gauge_ref, out_ref,
+    amp_ref, site_ref, weight_ref, recv, links, send_t, recv_t, stage, src,
+    in_sem, own_sem, g_send, g_recv, t_send, t_recv, f_send, f_recv,
 ):
     nz = groups * thick
     rows = 2 * nz
@@ -99,7 +99,12 @@
         )
         for i, (lo, n) in enumerate(parts)
     ]
-    for copy in own:
+    small = [
+        pltpu.make_async_copy(amp_hbm, amp_ref, in_sem.at[0]),
+        pltpu.make_async_copy(site_hbm, site_ref, in_sem.at[1]),
+        pltpu.make_async_copy(weight_hbm, weight_ref, in_sem.at[2]),
+    ]
+    for copy in small + own:
         copy.start()
 
     barrier = pltpu.get_barrier_semaphore()
@@ -176,6 +181,8 @@
             for i in range(6)
         )
 
+    for copy in small:
+        copy.wait()
     zero = jnp.zeros((rows, LANES), jnp.float32)
     fields = lax.fori_loop(0, points, add_point, (zero,) * 6)
     colour = (jnp.stack(fields[:3])[None], jnp.stack(fields[3:])[None])
@@ -307,19 +314,22 @@
     assert sides == groups and gauge.shape[4] == 1 and plane == 2 * LANES
     rows = 2 * thick * groups
     blocks = jnp.swapaxes(gauge.reshape(72, thick, 2, LANES), 1, 2).reshape(72, 2 * thick, LANES)
-    smem = pl.BlockSpec(memory_space=pltpu.SMEM)
     out = pl.pallas_call(
         functools.partial(kernel, groups, sheets, thick),
         out_shape=jax.ShapeDtypeStruct((sides, 2, 4, 3, 2 * thick, LANES), jnp.float32),
-        in_specs=[smem, smem, smem, pl.BlockSpec(memory_space=pl.ANY)],
+        in_specs=[pl.BlockSpec(memory_space=pl.ANY)] * 4,
         out_specs=pl.BlockSpec(memory_space=pl.ANY),
         scratch_shapes=[
+            pltpu.SMEM(amplitudes.shape, jnp.float32),
+            pltpu.SMEM(source_sites.shape, jnp.int32),
+            pltpu.SMEM(spin_weights.shape, jnp.float32),
             pltpu.VMEM((groups, 72, 2 * thick, LANES), jnp.float32),
             pltpu.VMEM((72, rows, LANES), jnp.float32),
             pltpu.VMEM((ITERS, 2, 2, 2, 3, rows, LANES), jnp.float32),
             pltpu.VMEM((ITERS, 2, 2, 2, 3, rows, LANES), jnp.float32),
             pltpu.VMEM((groups, 2, 4, 3, 2 * thick, LANES), jnp.float32),
             pltpu.VMEM((2, 4, 3, rows, LANES), jnp.float32),
+            pltpu.SemaphoreType.DMA((3,)),
             pltpu.SemaphoreType.DMA((3,)),
             pltpu.SemaphoreType.DMA((2, groups)),
             pltpu.SemaphoreType.DMA((2, groups)),
@@ -329,7 +339,7 @@
             pltpu.SemaphoreType.DMA((groups,)),
         ],
         compiler_params=pltpu.CompilerParams(
-            collective_id=0, has_side_effects=True, vmem_limit_bytes=32 * 1024 * 1024
+            collective_id=0, has_side_effects=True, vmem_limit_bytes=63 * 1024 * 1024
         ),
     )(amplitudes, source_sites, spin_weights, blocks)
     out = jnp.swapaxes(out.reshape(sides, 2, 4, 3, 2, thick, LANES), 4, 5)

time: 34 us -> 31.4 us (0.924)
  local copies, waits for them, and re-layouts: 3.6 us -> 1.54 us
  Pallas kernels: 30.2 us -> 29.7 us
    unnamed x9 -> x1, local copies, waits for them, and re-layouts: 3.6 us -> 1.54 us
    pallas_call x1, Pallas kernels: 30.2 us -> 29.7 us  [on_device(): pl.pallas_call(functools.partial(kernel, groups, sheets, thick), out_shap...]
where the time goes in v2:
time: 31.4 us; the launch traced here: 31.2 us
  Pallas kernels  29.7 us (95%)
  local copies, waits for them, and re-layouts  1.54 us (5%)
    pallas_call x1, Pallas kernels, on_device(): pl.pallas_call(functools.partial(kernel, groups, sheets, thick), out_shap...  29.7 us
    unnamed x1, local copies, waits for them, and re-layouts  1.54 us

profile of v2, /device:TPU:0, one launch (start us, length us, event | category | flops | bytes accessed | tf_op | source)
XLA Modules:
  0.0 31.2 jit_solution(11586313865119570103)
XLA Ops:
  0.0 29.7 %shard_map.46 = f32[2,2,4,3,4,128]{5,4,3,2,1,0:T(4,128)} custom-call(f32[2,2,3,1,32]{4,3,2,1,0:T(1,128)} %amp_hbm.1, s32[2,1,32]{2,1,0:T(1,128)} %site_hbm.1, f32[2,2,4]{2,1,0:T(2,128)} %weight_hbm.1, f32[72,4,128]{2,1,0:T(4,128)} %bitcast.11), custom_call_target="tpu_custom_call" | custom-call | tf_op jit(solution)/shard_map/pallas_call | solution.py:317
  29.7 1.5 %copy.8 = f32[2,2,4,3,1,2,256]{6,5,4,3,2,1,0:T(2,128)} copy(f32[2,2,4,3,1,2,256]{6,5,4,3,2,1,0:T(2,128)} %bitcast.10) | data formatting | bytes 196608

commit v3 on v2

--- a/solution.py
+++ b/solution.py
@@ -82,11 +82,13 @@
 
 def kernel(
     groups, sheets, thick, amp_hbm, site_hbm, weight_hbm, gauge_ref, out_ref,
-    amp_ref, site_ref, weight_ref, recv, links, send_t, recv_t, stage, src,
-    in_sem, own_sem, g_send, g_recv, t_send, t_recv, f_send, f_recv,
+    amp_ref, site_ref, weight_ref, recv, links, own_links, send_t, recv_t, send_z, recv_z,
+    stage, src, in_sem, own_sem, g_send, g_recv, t_send, t_recv, z_send, z_recv,
 ):
     nz = groups * thick
     rows = 2 * nz
+    sides = amp_ref.shape[0]
+    block = 2 * thick
     group = lax.axis_index("grp")
     sheet = lax.axis_index("lat")
     ahead = lax.rem(sheet + 1, sheets)
@@ -114,19 +116,18 @@
     pl.semaphore_signal(barrier, inc=1, device_id={"lat": behind})
     pl.semaphore_wait(barrier, groups + 1)
 
-    def gauge_copy(part, k, slot):
-        lo, n = parts[part]
+    def gauge_copy(k, slot):
+        lo, n = parts[0]
         return pltpu.make_async_remote_copy(
             src_ref=gauge_ref.at[pl.ds(lo, n)],
             dst_ref=recv.at[slot, pl.ds(lo, n)],
-            send_sem=g_send.at[part, k],
-            recv_sem=g_recv.at[part, k],
+            send_sem=g_send.at[k],
+            recv_sem=g_recv.at[k],
             device_id={"grp": lax.rem(group + k, groups)},
         )
 
-    for part in range(2):
-        for k in range(1, groups):
-            gauge_copy(part, k, group).start()
+    for k in range(1, groups):
+        gauge_copy(k, group).start()
 
     row = lax.broadcasted_iota(jnp.int32, (rows, LANES), 0)
     lane = lax.broadcasted_iota(jnp.int32, (rows, LANES), 1)
@@ -175,48 +176,52 @@
     points = site_ref.shape[2]
 
     def add_point(p, fields):
-        hit = cells == site_ref[group, 0, p]
+        hits = [cells == site_ref[side, 0, p] for side in range(sides)]
         return tuple(
-            fields[i] + jnp.where(hit, amp_ref[group, i // 3, i % 3, 0, p], 0.0)
-            for i in range(6)
+            fields[i] + jnp.where(hits[i // 6], amp_ref[i // 6, i // 3 % 2, i % 3, 0, p], 0.0)
+            for i in range(6 * sides)
         )
 
     for copy in small:
         copy.wait()
     zero = jnp.zeros((rows, LANES), jnp.float32)
-    fields = lax.fori_loop(0, points, add_point, (zero,) * 6)
-    colour = (jnp.stack(fields[:3])[None], jnp.stack(fields[3:])[None])
-
-    def arrange(part):
-        lo, n = parts[part]
-        own[part].wait()
-        for k in range(1, groups):
-            gauge_copy(part, k, lax.rem(group + groups - k, groups)).wait_recv()
-        for owner in range(groups):
-            for half in range(2):
-                to = half * nz + owner * thick
-                links[pl.ds(lo, n), to : to + thick, :] = recv[
-                    owner, pl.ds(lo, n), half * thick : (half + 1) * thick, :
-                ]
-
-    def link(hop_dir):
+    fields = lax.fori_loop(0, points, add_point, (zero,) * (6 * sides))
+    colour = tuple(
+        jnp.stack([jnp.stack(fields[6 * side + 3 * i :][:3]) for side in range(sides)])
+        for i in range(2)
+    )
+
+    for copy in own:
+        copy.wait()
+    for side in range(sides):
+        own_links[:, side * block : (side + 1) * block, :] = recv[group]
+    for k in range(1, groups):
+        gauge_copy(k, lax.rem(group + groups - k, groups)).wait_recv()
+    lo, n = parts[0]
+    for owner in range(groups):
+        for half in range(2):
+            to = half * nz + owner * thick
+            links[:, to : to + thick, :] = recv[
+                owner, lo : lo + n, half * thick : (half + 1) * thick, :
+            ]
+
+    def link(hop_dir, table):
         class View:
             def __getitem__(self, index):
                 base = hop_dir * 18 + index[0] * 9 + index[1] * 3
                 if len(index) == 3:
-                    return links[base + index[2]]
-                return links[base : base + 3]
+                    return table[base + index[2]]
+                return table[base : base + 3]
 
         return View()
 
-    arrange(0)
     norm = 1.0 + 6.0 * smear_weight
 
     def smear(_, colour):
         total = None
         for hop_dir in range(3):
-            fwd = times_link(link(hop_dir), shifted_pair(colour, hop_dir, 1), False)
-            back = shifted_pair(times_link(link(hop_dir), colour, True), hop_dir, -1)
+            fwd = times_link(link(hop_dir, links), shifted_pair(colour, hop_dir, 1), False)
+            back = shifted_pair(times_link(link(hop_dir, links), colour, True), hop_dir, -1)
             add = (fwd[0] + back[0], fwd[1] + back[1])
             total = add if total is None else (total[0] + add[0], total[1] + add[1])
         return tuple(
@@ -224,14 +229,67 @@
         )
 
     colour = lax.fori_loop(0, N_SMEAR, smear, colour)
-    c_re, c_im = colour[0][0], colour[1][0]
+    picked = []
+    for i in range(2):
+        pieces = []
+        for side in range(sides):
+            for half in range(2):
+                piece = None
+                for owner in range(groups):
+                    at = half * nz + owner * thick
+                    part = colour[i][side, :, at : at + thick, :]
+                    piece = part if piece is None else jnp.where(group == owner, part, piece)
+                pieces.append(piece)
+        picked.append(jnp.concatenate(pieces, axis=1))
+    c_re, c_im = picked
+    hrows = sides * block
+    hrow = lax.broadcasted_iota(jnp.int32, (hrows, LANES), 0)
+    hlane = lax.broadcasted_iota(jnp.int32, (hrows, LANES), 1)
+    hcol = hlane % LXY
+    hz = hrow % thick
+    low_half = hrow % block < thick
     for spin in range(4):
-        w_re = weight_ref[group, 0, spin]
-        w_im = weight_ref[group, 1, spin]
+        w_re = jnp.full((hrows, LANES), weight_ref[0, 0, spin], jnp.float32)
+        w_im = jnp.full((hrows, LANES), weight_ref[0, 1, spin], jnp.float32)
+        for side in range(1, sides):
+            w_re = jnp.where(hrow >= side * block, weight_ref[side, 0, spin], w_re)
+            w_im = jnp.where(hrow >= side * block, weight_ref[side, 1, spin], w_im)
         src[0, spin] = w_re * c_re - w_im * c_im
         src[1, spin] = w_re * c_im + w_im * c_re
 
-    arrange(1)
+    def hshift(field, hop_dir, offset):
+        lanes_axis, rows_axis = field.ndim - 1, field.ndim - 2
+        if hop_dir == 0:
+            fix = LXY - 1 if offset > 0 else LANES - LXY + 1
+            move = LANES - 1 if offset > 0 else 1
+            edge = hcol == (LXY - 1 if offset > 0 else 0)
+            return jnp.where(
+                edge, pltpu.roll(field, fix, lanes_axis), pltpu.roll(field, move, lanes_axis)
+            )
+        rolled = pltpu.roll(field, LANES - LXY if offset > 0 else LXY, lanes_axis)
+        edge = hlane >= LANES - LXY if offset > 0 else hlane < LXY
+        other = jnp.where(
+            low_half,
+            pltpu.roll(rolled, hrows - thick, rows_axis),
+            pltpu.roll(rolled, thick, rows_axis),
+        )
+        return jnp.where(edge, other, rolled)
+
+    def hshift_pair(pair, hop_dir, offset):
+        return hshift(pair[0], hop_dir, offset), hshift(pair[1], hop_dir, offset)
+
+    def z_copy(step, way):
+        by = groups - 1 if way == 0 else 1
+        return pltpu.make_async_remote_copy(
+            src_ref=send_z.at[step],
+            dst_ref=recv_z.at[step, way],
+            send_sem=z_send.at[step, way],
+            recv_sem=z_recv.at[step, way],
+            device_id={"grp": lax.rem(group + by, groups)},
+        )
+
+    z_ways = 1 if groups == 2 else 2
+
     sign_low = jnp.where(sheet == 0, -1.0, 1.0).astype(jnp.float32)
     sign_high = jnp.where(sheet == sheets - 1, -1.0, 1.0).astype(jnp.float32)
 
@@ -250,20 +308,46 @@
         send_t[step, 0, 0] = minus[0]
         send_t[step, 0, 1] = minus[1]
         t_copy(step, 0).start()
-        plus = times_link(link(3), project(3, 1, psi), True)
+        plus = times_link(link(3, own_links), project(3, 1, psi), True)
         send_t[step, 1, 0] = plus[0]
         send_t[step, 1, 1] = plus[1]
         t_copy(step, 1).start()
-        zeros = jnp.zeros((3, rows, LANES), jnp.float32)
+        z_ahead = project(2, -1, psi)
+        z_back = times_link(link(2, own_links), project(2, 1, psi), True)
+        for i in range(2):
+            send_z[step, i] = jnp.where(hz == 0, z_ahead[i], z_back[i])
+        for way in range(z_ways):
+            z_copy(step, way).start()
+        zeros = jnp.zeros((3, hrows, LANES), jnp.float32)
         total = ([zeros] * 4, [zeros] * 4)
-        for hop_dir in range(3):
-            half = shifted_pair(project(hop_dir, -1, psi), hop_dir, 1)
-            total = add_rows(hop_dir, -1, total, times_link(link(hop_dir), half, False))
-            half = times_link(link(hop_dir), project(hop_dir, 1, psi), True)
-            total = add_rows(hop_dir, 1, total, shifted_pair(half, hop_dir, -1))
+        for hop_dir in range(2):
+            half = hshift_pair(project(hop_dir, -1, psi), hop_dir, 1)
+            total = add_rows(hop_dir, -1, total, times_link(link(hop_dir, own_links), half, False))
+            half = times_link(link(hop_dir, own_links), project(hop_dir, 1, psi), True)
+            total = add_rows(hop_dir, 1, total, hshift_pair(half, hop_dir, -1))
+        for way in range(z_ways):
+            z_copy(step, way).wait_recv()
+        half = tuple(
+            jnp.where(
+                hz == thick - 1,
+                pltpu.roll(recv_z[step, 0, i], thick - 1, 2),
+                pltpu.roll(z_ahead[i], hrows - 1, 2),
+            )
+            for i in range(2)
+        )
+        total = add_rows(2, -1, total, times_link(link(2, own_links), half, False))
+        half = tuple(
+            jnp.where(
+                hz == 0,
+                pltpu.roll(recv_z[step, z_ways - 1, i], hrows - thick + 1, 2),
+                pltpu.roll(z_back[i], 1, 2),
+            )
+            for i in range(2)
+        )
+        total = add_rows(2, 1, total, half)
         t_copy(step, 0).wait_recv()
         half = (sign_high * recv_t[step, 0, 0], sign_high * recv_t[step, 0, 1])
-        total = add_rows(3, -1, total, times_link(link(3), half, False))
+        total = add_rows(3, -1, total, times_link(link(3, own_links), half, False))
         t_copy(step, 1).wait_recv()
         half = (sign_low * recv_t[step, 1, 0], sign_low * recv_t[step, 1, 1])
         total = add_rows(3, 1, total, half)
@@ -271,38 +355,19 @@
 
     psi = lax.fori_loop(0, ITERS, hop, (src[0], src[1]))
 
-    for owner in range(groups):
-        for half in range(2):
-            at = half * nz + owner * thick
-            for i in range(2):
-                stage[owner, i, :, :, half * thick : (half + 1) * thick, :] = psi[i][
-                    :, :, at : at + thick, :
-                ]
-
-    def final_copy(k, slot, to):
-        return pltpu.make_async_remote_copy(
-            src_ref=stage.at[slot],
-            dst_ref=out_ref.at[to],
-            send_sem=f_send.at[k],
-            recv_sem=f_recv.at[k],
-            device_id={"grp": lax.rem(group + k, groups)},
-        )
-
+    for side in range(sides):
+        for i in range(2):
+            stage[side, i] = psi[i][:, :, side * block : (side + 1) * block, :]
+    done = pltpu.make_async_copy(stage, out_ref, own_sem.at[2])
+    done.start()
     for k in range(1, groups):
-        final_copy(k, lax.rem(group + k, groups), group).start()
-    mine = pltpu.make_async_copy(stage.at[group], out_ref.at[group], own_sem.at[2])
-    mine.start()
-
-    for part in range(2):
-        for k in range(1, groups):
-            gauge_copy(part, k, group).wait_send()
+        gauge_copy(k, group).wait_send()
     for step in range(ITERS):
         for way in range(2):
             t_copy(step, way).wait_send()
-    mine.wait()
-    for k in range(1, groups):
-        final_copy(k, lax.rem(group + k, groups), group).wait_send()
-        final_copy(k, group, lax.rem(group + groups - k, groups)).wait_recv()
+        for way in range(z_ways):
+            z_copy(step, way).wait_send()
+    done.wait()
 
 
 def on_device(gauge, amplitudes, source_sites, spin_weights):
@@ -311,8 +376,9 @@
     thick = gauge.shape[5]
     plane = gauge.shape[6]
     sides = amplitudes.shape[0]
-    assert sides == groups and gauge.shape[4] == 1 and plane == 2 * LANES
+    assert groups > 1 and gauge.shape[4] == 1 and plane == 2 * LANES
     rows = 2 * thick * groups
+    hrows = 2 * thick * sides
     blocks = jnp.swapaxes(gauge.reshape(72, thick, 2, LANES), 1, 2).reshape(72, 2 * thick, LANES)
     out = pl.pallas_call(
         functools.partial(kernel, groups, sheets, thick),
@@ -324,19 +390,22 @@
             pltpu.SMEM(source_sites.shape, jnp.int32),
             pltpu.SMEM(spin_weights.shape, jnp.float32),
             pltpu.VMEM((groups, 72, 2 * thick, LANES), jnp.float32),
-            pltpu.VMEM((72, rows, LANES), jnp.float32),
-            pltpu.VMEM((ITERS, 2, 2, 2, 3, rows, LANES), jnp.float32),
-            pltpu.VMEM((ITERS, 2, 2, 2, 3, rows, LANES), jnp.float32),
-            pltpu.VMEM((groups, 2, 4, 3, 2 * thick, LANES), jnp.float32),
-            pltpu.VMEM((2, 4, 3, rows, LANES), jnp.float32),
+            pltpu.VMEM((54, rows, LANES), jnp.float32),
+            pltpu.VMEM((72, hrows, LANES), jnp.float32),
+            pltpu.VMEM((ITERS, 2, 2, 2, 3, hrows, LANES), jnp.float32),
+            pltpu.VMEM((ITERS, 2, 2, 2, 3, hrows, LANES), jnp.float32),
+            pltpu.VMEM((ITERS, 2, 2, 3, hrows, LANES), jnp.float32),
+            pltpu.VMEM((ITERS, 2, 2, 2, 3, hrows, LANES), jnp.float32),
+            pltpu.VMEM((sides, 2, 4, 3, 2 * thick, LANES), jnp.float32),
+            pltpu.VMEM((2, 4, 3, hrows, LANES), jnp.float32),
             pltpu.SemaphoreType.DMA((3,)),
             pltpu.SemaphoreType.DMA((3,)),
-            pltpu.SemaphoreType.DMA((2, groups)),
-            pltpu.SemaphoreType.DMA((2, groups)),
+            pltpu.SemaphoreType.DMA((groups,)),
+            pltpu.SemaphoreType.DMA((groups,)),
             pltpu.SemaphoreType.DMA((ITERS, 2)),
             pltpu.SemaphoreType.DMA((ITERS, 2)),
-            pltpu.SemaphoreType.DMA((groups,)),
-            pltpu.SemaphoreType.DMA((groups,)),
+            pltpu.SemaphoreType.DMA((ITERS, 2)),
+            pltpu.SemaphoreType.DMA((ITERS, 2)),
         ],
         compiler_params=pltpu.CompilerParams(
             collective_id=0, has_side_effects=True, vmem_limit_bytes=63 * 1024 * 1024

time: 31.4 us -> 30.1 us (0.959)
  Pallas kernels: 29.7 us -> 28.4 us
    pallas_call x1, Pallas kernels: 29.7 us -> 28.4 us  [on_device(): pl.pallas_call(functools.partial(kernel, groups, sheets, thick), out_shap...]
where the time goes in v3:
time: 30.1 us; the launch traced here: 30 us
  Pallas kernels  28.4 us (94%)
  local copies, waits for them, and re-layouts  1.54 us (5%)
    pallas_call x1, Pallas kernels, on_device(): pl.pallas_call(functools.partial(kernel, groups, sheets, thick), out_shap...  28.4 us
    unnamed x1, local copies, waits for them, and re-layouts  1.54 us

profile of v3, /device:TPU:0, one launch (start us, length us, event | category | flops | bytes accessed | tf_op | source)
XLA Modules:
  0.0 30.0 jit_solution(2066234790516516661)
XLA Ops:
  0.0 28.4 %shard_map.46 = f32[2,2,4,3,4,128]{5,4,3,2,1,0:T(4,128)} custom-call(f32[2,2,3,1,32]{4,3,2,1,0:T(1,128)} %amp_hbm.1, s32[2,1,32]{2,1,0:T(1,128)} %site_hbm.1, f32[2,2,4]{2,1,0:T(2,128)} %weight_hbm.1, f32[72,4,128]{2,1,0:T(4,128)} %bitcast.11), custom_call_target="tpu_custom_call" | custom-call | tf_op jit(solution)/shard_map/pallas_call | solution.py:383
  28.4 1.5 %copy.8 = f32[2,2,4,3,1,2,256]{6,5,4,3,2,1,0:T(2,128)} copy(f32[2,2,4,3,1,2,256]{6,5,4,3,2,1,0:T(2,128)} %bitcast.10) | data formatting | bytes 196608

commit v4 on v3

--- a/solution.py
+++ b/solution.py
@@ -83,7 +83,7 @@
 def kernel(
     groups, sheets, thick, amp_hbm, site_hbm, weight_hbm, gauge_ref, out_ref,
     amp_ref, site_ref, weight_ref, recv, links, own_links, send_t, recv_t, send_z, recv_z,
-    stage, src, in_sem, own_sem, g_send, g_recv, t_send, t_recv, z_send, z_recv,
+    src, in_sem, own_sem, g_send, g_recv, t_send, t_recv, z_send, z_recv,
 ):
     nz = groups * thick
     rows = 2 * nz
@@ -357,9 +357,7 @@
 
     for side in range(sides):
         for i in range(2):
-            stage[side, i] = psi[i][:, :, side * block : (side + 1) * block, :]
-    done = pltpu.make_async_copy(stage, out_ref, own_sem.at[2])
-    done.start()
+            out_ref[side, i] = psi[i][:, :, side * block : (side + 1) * block, :]
     for k in range(1, groups):
         gauge_copy(k, group).wait_send()
     for step in range(ITERS):
@@ -367,7 +365,6 @@
             t_copy(step, way).wait_send()
         for way in range(z_ways):
             z_copy(step, way).wait_send()
-    done.wait()
 
 
 def on_device(gauge, amplitudes, source_sites, spin_weights):
@@ -382,9 +379,9 @@
     blocks = jnp.swapaxes(gauge.reshape(72, thick, 2, LANES), 1, 2).reshape(72, 2 * thick, LANES)
     out = pl.pallas_call(
         functools.partial(kernel, groups, sheets, thick),
-        out_shape=jax.ShapeDtypeStruct((sides, 2, 4, 3, 2 * thick, LANES), jnp.float32),
+        out_shape=pltpu.VMEM((sides, 2, 4, 3, 2 * thick, LANES), jnp.float32),
         in_specs=[pl.BlockSpec(memory_space=pl.ANY)] * 4,
-        out_specs=pl.BlockSpec(memory_space=pl.ANY),
+        out_specs=pl.BlockSpec(memory_space=pltpu.VMEM),
         scratch_shapes=[
             pltpu.SMEM(amplitudes.shape, jnp.float32),
             pltpu.SMEM(source_sites.shape, jnp.int32),
@@ -396,10 +393,9 @@
             pltpu.VMEM((ITERS, 2, 2, 2, 3, hrows, LANES), jnp.float32),
             pltpu.VMEM((ITERS, 2, 2, 3, hrows, LANES), jnp.float32),
             pltpu.VMEM((ITERS, 2, 2, 2, 3, hrows, LANES), jnp.float32),
-            pltpu.VMEM((sides, 2, 4, 3, 2 * thick, LANES), jnp.float32),
             pltpu.VMEM((2, 4, 3, hrows, LANES), jnp.float32),
             pltpu.SemaphoreType.DMA((3,)),
-            pltpu.SemaphoreType.DMA((3,)),
+            pltpu.SemaphoreType.DMA((2,)),
             pltpu.SemaphoreType.DMA((groups,)),
             pltpu.SemaphoreType.DMA((groups,)),
             pltpu.SemaphoreType.DMA((ITERS, 2)),

time: 30.1 us -> 28.6 us (0.950)
  local copies, waits for them, and re-layouts: 1.54 us -> 0.64 us
  Pallas kernels: 28.4 us -> 27.8 us
    unnamed x1, local copies, waits for them, and re-layouts: 1.54 us -> 0.64 us
    pallas_call x1, Pallas kernels: 28.4 us -> 27.8 us  [on_device(): pl.pallas_call(functools.partial(kernel, groups, sheets, thick), out_shap...]
where the time goes in v4:
time: 28.6 us; the launch traced here: 28.5 us
  Pallas kernels  27.8 us (97%)
  local copies, waits for them, and re-layouts  0.64 us (2%)
    pallas_call x1, Pallas kernels, on_device(): pl.pallas_call(functools.partial(kernel, groups, sheets, thick), out_shap...  27.8 us
    unnamed x1, local copies, waits for them, and re-layouts  0.64 us

profile of v4, /device:TPU:0, one launch (start us, length us, event | category | flops | bytes accessed | tf_op | source)
XLA Modules:
  0.0 28.5 jit_solution(4885473178949734785)
XLA Ops:
  0.0 27.8 %shard_map.46 = f32[2,2,4,3,4,128]{5,4,3,2,1,0:T(4,128)S(1)} custom-call(f32[2,2,3,1,32]{4,3,2,1,0:T(1,128)} %amp_hbm.1, s32[2,1,32]{2,1,0:T(1,128)} %site_hbm.1, f32[2,2,4]{2,1,0:T(2,128)} %weight_hbm.1, f32[72,4,128]{2,1,0:T(4,128)} %bitcast.11), custom_call_target="tpu_custom_call" | custom-call | tf_op jit(solution)/shard_map/pallas_call | solution.py:380
  27.8 0.6 %copy.8 = f32[2,2,4,3,1,2,256]{6,5,4,3,2,1,0:T(2,128)} copy(f32[2,2,4,3,1,2,256]{6,5,4,3,2,1,0:T(2,128)S(1)} %bitcast.10) | data formatting | bytes 196608

commit v5 on v4

--- a/solution.py
+++ b/solution.py
@@ -116,18 +116,19 @@
     pl.semaphore_signal(barrier, inc=1, device_id={"lat": behind})
     pl.semaphore_wait(barrier, groups + 1)
 
-    def gauge_copy(k, slot):
-        lo, n = parts[0]
+    def gauge_copy(k, slot, hop_dir):
+        lo, n = 18 * hop_dir, 18
         return pltpu.make_async_remote_copy(
             src_ref=gauge_ref.at[pl.ds(lo, n)],
             dst_ref=recv.at[slot, pl.ds(lo, n)],
-            send_sem=g_send.at[k],
-            recv_sem=g_recv.at[k],
+            send_sem=g_send.at[hop_dir, k],
+            recv_sem=g_recv.at[hop_dir, k],
             device_id={"grp": lax.rem(group + k, groups)},
         )
 
     for k in range(1, groups):
-        gauge_copy(k, group).start()
+        for hop_dir in range(3):
+            gauge_copy(k, group, hop_dir).start()
 
     row = lax.broadcasted_iota(jnp.int32, (rows, LANES), 0)
     lane = lax.broadcasted_iota(jnp.int32, (rows, LANES), 1)
@@ -196,7 +197,8 @@
     for side in range(sides):
         own_links[:, side * block : (side + 1) * block, :] = recv[group]
     for k in range(1, groups):
-        gauge_copy(k, lax.rem(group + groups - k, groups)).wait_recv()
+        for hop_dir in range(3):
+            gauge_copy(k, lax.rem(group + groups - k, groups), hop_dir).wait_recv()
     lo, n = parts[0]
     for owner in range(groups):
         for half in range(2):
@@ -293,25 +295,25 @@
     sign_low = jnp.where(sheet == 0, -1.0, 1.0).astype(jnp.float32)
     sign_high = jnp.where(sheet == sheets - 1, -1.0, 1.0).astype(jnp.float32)
 
-    def t_copy(step, way):
+    def t_copy(step, way, i):
         return pltpu.make_async_remote_copy(
-            src_ref=send_t.at[step, way],
-            dst_ref=recv_t.at[step, way],
-            send_sem=t_send.at[step, way],
-            recv_sem=t_recv.at[step, way],
+            src_ref=send_t.at[step, way, i],
+            dst_ref=recv_t.at[step, way, i],
+            send_sem=t_send.at[step, way, i],
+            recv_sem=t_recv.at[step, way, i],
             device_id={"lat": behind if way == 0 else ahead},
         )
 
     def hop(step, psi):
         psi = (psi[0], psi[1])
         minus = project(3, -1, psi)
-        send_t[step, 0, 0] = minus[0]
-        send_t[step, 0, 1] = minus[1]
-        t_copy(step, 0).start()
+        for i in range(2):
+            send_t[step, 0, i] = minus[i]
+            t_copy(step, 0, i).start()
         plus = times_link(link(3, own_links), project(3, 1, psi), True)
-        send_t[step, 1, 0] = plus[0]
-        send_t[step, 1, 1] = plus[1]
-        t_copy(step, 1).start()
+        for i in range(2):
+            send_t[step, 1, i] = plus[i]
+            t_copy(step, 1, i).start()
         z_ahead = project(2, -1, psi)
         z_back = times_link(link(2, own_links), project(2, 1, psi), True)
         for i in range(2):
@@ -345,10 +347,12 @@
             for i in range(2)
         )
         total = add_rows(2, 1, total, half)
-        t_copy(step, 0).wait_recv()
+        for i in range(2):
+            t_copy(step, 0, i).wait_recv()
         half = (sign_high * recv_t[step, 0, 0], sign_high * recv_t[step, 0, 1])
         total = add_rows(3, -1, total, times_link(link(3, own_links), half, False))
-        t_copy(step, 1).wait_recv()
+        for i in range(2):
+            t_copy(step, 1, i).wait_recv()
         half = (sign_low * recv_t[step, 1, 0], sign_low * recv_t[step, 1, 1])
         total = add_rows(3, 1, total, half)
         return tuple(src[i] + hop_kappa * jnp.stack(total[i]) for i in range(2))
@@ -359,10 +363,12 @@
         for i in range(2):
             out_ref[side, i] = psi[i][:, :, side * block : (side + 1) * block, :]
     for k in range(1, groups):
-        gauge_copy(k, group).wait_send()
+        for hop_dir in range(3):
+            gauge_copy(k, group, hop_dir).wait_send()
     for step in range(ITERS):
         for way in range(2):
-            t_copy(step, way).wait_send()
+            for i in range(2):
+                t_copy(step, way, i).wait_send()
         for way in range(z_ways):
             z_copy(step, way).wait_send()
 
@@ -396,10 +402,10 @@
             pltpu.VMEM((2, 4, 3, hrows, LANES), jnp.float32),
             pltpu.SemaphoreType.DMA((3,)),
             pltpu.SemaphoreType.DMA((2,)),
-            pltpu.SemaphoreType.DMA((groups,)),
-            pltpu.SemaphoreType.DMA((groups,)),
-            pltpu.SemaphoreType.DMA((ITERS, 2)),
-            pltpu.SemaphoreType.DMA((ITERS, 2)),
+            pltpu.SemaphoreType.DMA((3, groups)),
+            pltpu.SemaphoreType.DMA((3, groups)),
+            pltpu.SemaphoreType.DMA((ITERS, 2, 2)),
+            pltpu.SemaphoreType.DMA((ITERS, 2, 2)),
             pltpu.SemaphoreType.DMA((ITERS, 2)),
             pltpu.SemaphoreType.DMA((ITERS, 2)),
         ],

time: 28.6 us -> 28.8 us (level)
  no operation moved by 1% of the time
where the time goes in v5:
time: 28.8 us; the launch traced here: 28.7 us
  Pallas kernels  28 us (97%)
  local copies, waits for them, and re-layouts  0.64 us (2%)
    pallas_call x1, Pallas kernels, on_device(): pl.pallas_call(functools.partial(kernel, groups, sheets, thick), out_shap...  28 us
    unnamed x1, local copies, waits for them, and re-layouts  0.64 us

profile of v5, /device:TPU:0, one launch (start us, length us, event | category | flops | bytes accessed | tf_op | source)
XLA Modules:
  0.0 28.7 jit_solution(3556417081387992603)
XLA Ops:
  0.0 28.0 %shard_map.46 = f32[2,2,4,3,4,128]{5,4,3,2,1,0:T(4,128)S(1)} custom-call(f32[2,2,3,1,32]{4,3,2,1,0:T(1,128)} %amp_hbm.1, s32[2,1,32]{2,1,0:T(1,128)} %site_hbm.1, f32[2,2,4]{2,1,0:T(2,128)} %weight_hbm.1, f32[72,4,128]{2,1,0:T(4,128)} %bitcast.11), custom_call_target="tpu_custom_call" | custom-call | tf_op jit(solution)/shard_map/pallas_call | solution.py:386
  28.0 0.6 %copy.8 = f32[2,2,4,3,1,2,256]{6,5,4,3,2,1,0:T(2,128)} copy(f32[2,2,4,3,1,2,256]{6,5,4,3,2,1,0:T(2,128)S(1)} %bitcast.10) | data formatting | bytes 196608

commit v6 on v4

--- a/solution.py
+++ b/solution.py
@@ -228,7 +228,7 @@
             (1.0 / norm) * colour[i] + (smear_weight / norm) * total[i] for i in range(2)
         )
 
-    colour = lax.fori_loop(0, N_SMEAR, smear, colour)
+    colour = lax.fori_loop(0, N_SMEAR, smear, colour, unroll=True)
     picked = []
     for i in range(2):
         pieces = []
@@ -353,7 +353,7 @@
         total = add_rows(3, 1, total, half)
         return tuple(src[i] + hop_kappa * jnp.stack(total[i]) for i in range(2))
 
-    psi = lax.fori_loop(0, ITERS, hop, (src[0], src[1]))
+    psi = lax.fori_loop(0, ITERS, hop, (src[0], src[1]), unroll=True)
 
     for side in range(sides):
         for i in range(2):

time: 28.6 us -> 28.5 us (level)
  no operation moved by 1% of the time
where the time goes in v6:
time: 28.5 us; the launch traced here: 28.3 us
  Pallas kernels  27.7 us (97%)
  local copies, waits for them, and re-layouts  0.64 us (2%)
    pallas_call x1, Pallas kernels, on_device(): pl.pallas_call(functools.partial(kernel, groups, sheets, thick), out_shap...  27.7 us
    unnamed x1, local copies, waits for them, and re-layouts  0.64 us

profile of v6, /device:TPU:0, one launch (start us, length us, event | category | flops | bytes accessed | tf_op | source)
XLA Modules:
  0.0 28.3 jit_solution(3572630704416785076)
XLA Ops:
  0.0 27.7 %shard_map.46 = f32[2,2,4,3,4,128]{5,4,3,2,1,0:T(4,128)S(1)} custom-call(f32[2,2,3,1,32]{4,3,2,1,0:T(1,128)} %amp_hbm.1, s32[2,1,32]{2,1,0:T(1,128)} %site_hbm.1, f32[2,2,4]{2,1,0:T(2,128)} %weight_hbm.1, f32[72,4,128]{2,1,0:T(4,128)} %bitcast.11), custom_call_target="tpu_custom_call" | custom-call | tf_op jit(solution)/shard_map/pallas_call | solution.py:380
  27.7 0.6 %copy.8 = f32[2,2,4,3,1,2,256]{6,5,4,3,2,1,0:T(2,128)} copy(f32[2,2,4,3,1,2,256]{6,5,4,3,2,1,0:T(2,128)S(1)} %bitcast.10) | data formatting | bytes 196608
